TPU v7x, 256 devices: a whole 4x4x8 slice. The times are simulated.
256 devices in a mesh: dp: 32 (over z, x), tensor: 8 (over y, core).
Axes of the slice: x: 4, y: 4, z: 8, core: 2. Of those that a mesh axis runs over, the one named last changes fastest.
Arguments:
- momentum: float32 [32, 256, 28672], P('dp', None, 'tensor')
- gradient: bfloat16 [32, 256, 28672], P('dp', None, 'tensor'), may hold values from -6 to 6
- kept: int32 [32, 4, 448, 32], P('dp', None, 'tensor'), may hold values from 0 to 4095, as said below
Outputs:
- update: float32 [256, 28672], P(None, 'tensor')
- new_momentum: float32 [32, 256, 28672], P('dp', None, 'tensor')
Inputs may be any that keep to these rules, and one draw needn't show every extreme that they name: Sorted, the i-th kept index of a block lies in [i * 64 * 2, (i + 1) * 64 * 2); the kept indices of a block are distinct.
All inputs are finite; a program needn't handle non-finite values.
Results may differ from a plain program's by a relative error of at most 0.0003.
Values sent between devices are 32-bit elements; how exact they have to be, the bound alone decides.
No kernel may reach another device: no remote copies, remote signals or barrier semaphores. Data moves between devices by JAX's collectives and lax.ppermute only.
A program may use at most 128 MiB of HBM per device.

v0:
```python
import functools

import jax
import jax.numpy as jnp
import numpy as np
from jax import lax
from jax.experimental import pallas as pl
from jax.experimental.pallas import tpu as pltpu
from jax.sharding import PartitionSpec as P

FF = 28672
ROWS = 256
BLK = 64
KEEP = 32
BAND = BLK * BLK // KEEP
TILE = 256
WIDE = 1792

decay_rate = 0.9
epsilon = 1e-06


def thirds_np(x):
    high = x.astype(jnp.bfloat16)
    low = (x - high.astype(np.float32)).astype(jnp.bfloat16)
    return np.concatenate([high, low, high])


def constants():
    k = np.arange(BLK)[:, None]
    n = np.arange(BLK)[None, :]
    c = np.cos(np.pi * (2.0 * n + 1.0) * k / (2.0 * BLK)) * np.sqrt(2.0 / BLK)
    c[0] *= 1.0 / np.sqrt(2.0)
    right = np.kron(np.eye(4), c).astype(np.float32)
    order = [p * BLK + 2 * i + h for h in range(2) for p in range(4) for i in range(KEEP)]
    left = right[order]
    forward = np.stack([thirds_np(right.T), thirds_np(left.T)])
    inverse = np.stack([thirds_np(left), thirds_np(right)])
    return forward, inverse


def dot3(x, thirds):
    high = x.astype(jnp.bfloat16)
    low = (x - high.astype(jnp.float32)).astype(jnp.bfloat16)
    return jnp.dot(jnp.concatenate([high, high, low], axis=1), thirds, preferred_element_type=jnp.float32)


def tile(i):
    return slice(i * TILE, (i + 1) * TILE)


def block(q):
    return slice(q * BLK, (q + 1) * BLK)


def field(m_ref, g_ref, i):
    return decay_rate * m_ref[0, :, tile(i)] + g_ref[0, :, tile(i)].astype(jnp.float32)


def both_sides(x, c_ref):
    return dot3(dot3(x, c_ref[0]).T, c_ref[1])


def cells_of():
    cells = lax.broadcasted_iota(jnp.int32, (BLK, 128), 0).astype(jnp.float32)
    return cells, cells + float(BLK)


def values_kernel(m_ref, g_ref, e_ref, c_ref, p_ref):
    first = pl.program_id(0) * (WIDE // BLK)
    cells = cells_of()
    for i in range(WIDE // TILE):
        coeffs = both_sides(field(m_ref, g_ref, i), c_ref)
        for q in range(4):
            row = pl.ds(first + i * 4 + q, 1)
            e = e_ref[row, :]
            own = coeffs[block(q)]
            chosen = jnp.where(e == cells[0], own[:, :128], 0.0) + jnp.where(e == cells[1], own[:, 128:], 0.0)
            p_ref[0, row, :] = e
            p_ref[1, row, :] = jnp.sum(chosen, axis=0, keepdims=True)


def residual_kernel(m_ref, g_ref, p_ref, c_ref, o_ref):
    first = pl.program_id(0) * (WIDE // BLK)
    cells = cells_of()
    for i in range(WIDE // TILE):
        parts = []
        for q in range(4):
            row = pl.ds(first + i * 4 + q, 1)
            e, v = p_ref[0, row, :], p_ref[1, row, :]
            parts.append(jnp.concatenate([jnp.where(e == cell, v, 0.0) for cell in cells], axis=1))
        sent = both_sides(jnp.concatenate(parts, axis=0), c_ref)
        o_ref[0, :, tile(i)] = field(m_ref, g_ref, i) - sent


def merge_kernel(*refs, late):
    *parts, p_ref, sq_ref = refs
    held = replicas_of(parts)

    def rows(g, squares):
        at = pl.ds(pl.multiple_of(g * 8, 8), 8)
        places = [ref[r, 0, at, :] for ref, r in held]
        values = [ref[r, 1, at, :] for ref, r in held]
        for i in range(len(held)):
            place, total = places[i], values[i]
            for j in range(i + 1, len(held)):
                if j == late:
                    p_ref[i, 0, at, :] = place
                    p_ref[i, 1, at, :] = total
                same = place == places[j]
                total = total + jnp.where(same, values[j], 0.0)
                places[j] = jnp.where(same, -1.0 - j, places[j])
            squares = squares + jnp.where(place >= 0.0, total * total, 0.0)
        return squares

    sq_ref[...] = lax.fori_loop(0, p_ref.shape[2] // 8, rows, jnp.zeros((8, 128), jnp.float32))


def replicas_of(parts):
    return [(ref, r) for ref in parts for r in range(ref.shape[0])]


def summed_row(held, row, cell, distinct):
    total = jnp.zeros((BLK, 128), jnp.float32)
    for ref, r in held:
        here = ref[r, 0, row, :] == cell
        value = ref[r, 1, row, :]
        total = jnp.where(here, value, total) if distinct else total + jnp.where(here, value, 0.0)
    return total


def early_kernel(*refs):
    *parts, s_ref = refs
    held = replicas_of(parts)
    first = pl.program_id(0) * (WIDE // BLK)
    cells = cells_of()

    @pl.loop(0, WIDE // BLK)
    def _(q):
        rows = pl.ds(pl.multiple_of(q * BLK, BLK), BLK)
        for half in range(2):
            s_ref[rows, half * 128 : half * 128 + 128] = summed_row(held, pl.ds(first + q, 1), cells[half], False)


def late_kernel(p_ref, before_ref, c_ref, o_ref):
    held = replicas_of([p_ref])
    first = pl.program_id(0) * (WIDE // BLK)
    cells = cells_of()
    for i in range(WIDE // TILE):
        parts = []
        for q in range(4):
            row = pl.ds(first + i * 4 + q, 1)
            parts.append(jnp.concatenate([summed_row(held, row, cell, True) for cell in cells], axis=1))
        summed = before_ref[tile(i), :] + jnp.concatenate(parts, axis=0)
        o_ref[:, tile(i)] = both_sides(summed, c_ref)


def scale_kernel(x_ref, total_ref, o_ref):
    mean = jnp.sum(total_ref[...], keepdims=True) / (ROWS * FF)
    o_ref[...] = x_ref[...] * lax.rsqrt(mean + epsilon)


Z, X, T = 8, 4, 8


def tensor_sum(x):
    x = x + lax.ppermute(x, "tensor", [(t, t ^ 1) for t in range(T)])
    return x + sum(lax.ppermute(x, "tensor", [(t, (t + k) % T) for t in range(T)]) for k in (2, 6, 4))


def shift(x, dz, dx):
    pairs = [(z * X + c, (z + dz) % Z * X + (c + dx) % X) for z in range(Z) for c in range(X)]
    return lax.ppermute(x, "dp", pairs)


VMEM_LIMIT = 32 * 1024 * 1024
MIDDLE = 44 * 1024 * 1024
BIG = 60 * 1024 * 1024


def params(limit=VMEM_LIMIT):
    return pltpu.CompilerParams(vmem_limit_bytes=limit)


def cost(us):
    return pl.CostEstimate(flops=int(us * 1e9), bytes_accessed=int(us * 3.5e6), transcendentals=0)


def whole(shape):
    return pl.BlockSpec(shape, lambda j: (0,) * len(shape))


def across(x):
    return [shift(x, 0, k) for k in (1, 3, 2)]


def shards(momentum, gradient, kept):
    forward, inverse = constants()
    width = momentum.shape[2]
    steps = width // WIDE
    blocks = width // BLK
    band = jnp.arange(KEEP, dtype=jnp.int32) * BAND
    offsets = jnp.transpose(kept[0] - band, (1, 0, 2)).reshape(blocks, 128).astype(jnp.float32)
    field_spec = pl.BlockSpec((1, ROWS, WIDE), lambda j: (0, 0, j))
    const_spec = whole(forward.shape)
    packet_spec = whole((2, blocks, 128))
    packet = pl.pallas_call(
        values_kernel,
        grid=(steps,),
        in_specs=[field_spec, field_spec, whole((blocks, 128)), const_spec],
        out_specs=packet_spec,
        out_shape=jax.ShapeDtypeStruct((2, blocks, 128), jnp.float32),
        compiler_params=params(BIG),
        cost_estimate=cost(8),
    )(momentum, gradient, offsets, forward)
    three = jnp.stack([shift(packet, 1, 0), packet, shift(packet, -1, 0)])
    far = [shift(three, 3, 0), shift(three[:2], -3, 0)]
    three_x = across(three)
    packet, three = lax.optimization_barrier((packet, three))
    residual = pl.pallas_call(
        residual_kernel,
        grid=(steps,),
        in_specs=[field_spec, field_spec, packet_spec, const_spec],
        out_specs=field_spec,
        out_shape=jax.ShapeDtypeStruct(momentum.shape, jnp.float32),
        compiler_params=params(MIDDLE),
        cost_estimate=cost(8),
    )(momentum, gradient, packet, inverse)
    residual, *far = lax.optimization_barrier((residual, *far))
    five = jnp.concatenate(far)
    five_x = across(five)
    sum_spec = pl.BlockSpec((WIDE, TILE), lambda j: (j, 0))
    early = [three, *three_x, five]
    summed = pl.pallas_call(
        early_kernel,
        grid=(steps,),
        in_specs=[whole(x.shape) for x in early],
        out_specs=sum_spec,
        out_shape=jax.ShapeDtypeStruct((width, TILE), jnp.float32),
        compiler_params=params(),
        cost_estimate=cost(7),
    )(*early)
    summed, *five_x = lax.optimization_barrier((summed, *five_x))
    late = sum(x.shape[0] for x in five_x)
    merged, squares = pl.pallas_call(
        functools.partial(merge_kernel, late=late),
        out_shape=(
            jax.ShapeDtypeStruct((late, 2, blocks, 128), jnp.float32),
            jax.ShapeDtypeStruct((8, 128), jnp.float32),
        ),
        compiler_params=params(),
        cost_estimate=cost(2),
    )(*five_x, *early)
    total = tensor_sum(squares)
    combined = pl.pallas_call(
        late_kernel,
        grid=(steps,),
        in_specs=[whole(merged.shape), sum_spec, const_spec],
        out_specs=pl.BlockSpec((ROWS, WIDE), lambda j: (0, j)),
        out_shape=jax.ShapeDtypeStruct((ROWS, width), jnp.float32),
        compiler_params=params(),
        cost_estimate=cost(9),
    )(merged, summed, inverse)
    combined, total = lax.optimization_barrier((combined, total))
    scale_spec = pl.BlockSpec((64, width), lambda j: (j, 0))
    update = pl.pallas_call(
        scale_kernel,
        grid=(ROWS // 64,),
        in_specs=[scale_spec, whole((8, 128))],
        out_specs=scale_spec,
        out_shape=jax.ShapeDtypeStruct((ROWS, width), jnp.float32),
        compiler_params=params(),
        cost_estimate=cost(2),
    )(combined, total)
    return (update, residual)


def solution(mesh):
    return jax.shard_map(
        shards,
        mesh=mesh,
        in_specs=(P("dp", None, "tensor"), P("dp", None, "tensor"), P("dp", None, "tensor", None)),
        out_specs=(P(None, "tensor"), P("dp", None, "tensor")),
        check_vma=False,
    )
```

profile of v0, /device:TPU:32, one launch (start us, length us, event | category | flops | bytes accessed | tf_op | source)
XLA Modules:
  0.0 71.5 jit_solution(11244769970622109390)
XLA Ops:
  0.6 0.9 %fusion = f32[4,56,32]{1,2,0:T(8,128)S(1)} fusion(s32[1,4,56,32]{2,3,1,0:T(8,128)} %param.7, s32[32]{0:T(128)S(1)} %iota_multiply_fusion), kind=kLoop, calls=%fused_computation.3 | loop fusion | flops 14336 | bytes 57472 | tf_op jit(solution)/shard_map/convert_element_type | solution.py:203
  1.6 0.7 copy.8.e_ref
  2.3 6.7 %shard_map.68.p_ref = f32[2,56,128]{2,1,0:T(8,128)} custom-call(f32[1,256,3584]{2,1,0:T(8,128)} %m_ref.3, bf16[1,256,3584]{2,1,0:T(8,128)(2,1)} %g_ref.3, f32[56,128]{1,0:T(8,128)} %copy.8.e_ref, bf16[2,768,256]{2,1,0:T(8,128)(2,1)} %constant.6.clone.c_ref), custom_call_target="tpu_custom_call" | custom-call | flops 8000000000 | bytes 28000000 | tf_op jit(solution)/shard_map/pallas_call | solution.py:207
  8.9 1.9 %collective-permute-start = (f32[2,56,128]{2,1,0:T(8,128)}, f32[2,56,128]{2,1,0:T(8,128)S(1)}, u32[]{:S(2)}, u32[]{:S(2)}) collective-permute-start(f32[2,56,128]{2,1,0:T(8,128)} %shard_map.68.p_ref), channel_id=1, source_target_pairs={{0,32},{8,40},{16,48},{24,56},{32,64},{40,72},{48,80},{56,88},{64,... | collective-permute-start | bytes 172040 | tf_op jit(solution)/shard_map/ppermute | solution.py:173
  10.8 0.1 collective-permute-start.1
  10.9 2.4 %collective-permute-done = f32[2,56,128]{2,1,0:T(8,128)S(1)} collective-permute-done((f32[2,56,128]{2,1,0:T(8,128)}, f32[2,56,128]{2,1,0:T(8,128)S(1)}, u32[]{:S(2)}, u32[]{:S(2)}) %collective-permute-start) | collective-permute-done | bytes 57376 | tf_op jit(solution)/shard_map/ppermute | solution.py:173
  13.3 0.8 %pad_maximum_fusion.1 = f32[2,2,56,128]{3,2,1,0:T(8,128)S(1)} fusion(f32[1,2,56,128]{3,2,1,0:T(8,128)} %bitcast.10, f32[1,2,56,128]{3,2,1,0:T(8,128)S(1)} %bitcast.13), kind=kLoop, calls=%fused_computation.1 | loop fusion | flops 28672 | bytes 229376 | tf_op jit(solution)/shard_map/stack | solution.py:216
  14.1 1.1 %collective-permute-done.1 = f32[2,56,128]{2,1,0:T(8,128)S(1)} collective-permute-done((f32[2,56,128]{2,1,0:T(8,128)}, f32[2,56,128]{2,1,0:T(8,128)S(1)}, u32[]{:S(2)}, u32[]{:S(2)}) %collective-permute-start.1) | collective-permute-done | bytes 57376 | tf_op jit(solution)/shard_map/ppermute | solution.py:173
  15.2 0.8 %pad_maximum_fusion.refs_0_.refs_3_ = f32[3,2,56,128]{3,2,1,0:T(8,128)S(1)} fusion(f32[1,2,56,128]{3,2,1,0:T(8,128)S(1)} %bitcast.15, f32[1,2,56,128]{3,2,1,0:T(8,128)} %bitcast.11, f32[1,2,56,128]{3,2,1,0:T(8,128)S(1)} %bitcast.14), kind=kLoop, calls=%fused_computation | loop fusion | flops 86016 | bytes 344064 | tf_op jit(solution)/shard_map/stack | solution.py:216
  16.0 6.0 %collective-permute-start.5 = (f32[3,2,56,128]{3,2,1,0:T(8,128)S(1)}, f32[3,2,56,128]{3,2,1,0:T(8,128)S(1)}, u32[]{:S(2)}, u32[]{:S(2)}) collective-permute-start(f32[3,2,56,128]{3,2,1,0:T(8,128)S(1)} %pad_maximum_fusion.refs_0_.refs_3_), channel_id=1, source_target_pairs={{0,96},{8,104},{16,112},{24,120},{32,128},{40,136},{48,144},{56,15... | collective-permute-start | bytes 516104 | tf_op jit(solution)/shard_map/ppermute | solution.py:173
  22.1 3.0 %collective-permute-start.4 = (f32[3,2,56,128]{3,2,1,0:T(8,128)S(1)}, f32[3,2,56,128]{3,2,1,0:T(8,128)S(1)}, u32[]{:S(2)}, u32[]{:S(2)}) collective-permute-start(f32[3,2,56,128]{3,2,1,0:T(8,128)S(1)} %pad_maximum_fusion.refs_0_.refs_3_), channel_id=1, source_target_pairs={{0,16},{8,24},{16,0},{24,8},{32,48},{40,56},{48,32},{56,40},{64,80... | collective-permute-start | bytes 516104 | tf_op jit(solution)/shard_map/ppermute | solution.py:173
  25.1 1.1 %collective-permute-start.3 = (f32[3,2,56,128]{3,2,1,0:T(8,128)S(1)}, f32[3,2,56,128]{3,2,1,0:T(8,128)S(1)}, u32[]{:S(2)}, u32[]{:S(2)}) collective-permute-start(f32[3,2,56,128]{3,2,1,0:T(8,128)S(1)} %pad_maximum_fusion.refs_0_.refs_3_), channel_id=1, source_target_pairs={{0,24},{8,0},{16,8},{24,16},{32,56},{40,32},{48,40},{56,48},{64,88... | collective-permute-start | bytes 516104 | tf_op jit(solution)/shard_map/ppermute | solution.py:173
  26.3 0.9 %collective-permute-start.2 = (f32[3,2,56,128]{3,2,1,0:T(8,128)S(1)}, f32[3,2,56,128]{3,2,1,0:T(8,128)S(1)}, u32[]{:S(2)}, u32[]{:S(2)}) collective-permute-start(f32[3,2,56,128]{3,2,1,0:T(8,128)S(1)} %pad_maximum_fusion.refs_0_.refs_3_), channel_id=1, source_target_pairs={{0,8},{8,16},{16,24},{24,0},{32,40},{40,48},{48,56},{56,32},{64,72... | collective-permute-start | bytes 516104 | tf_op jit(solution)/shard_map/ppermute | solution.py:173
  27.2 0.8 %copy-done = f32[2,56,128]{2,1,0:T(8,128)S(1)} copy-done((f32[2,56,128]{2,1,0:T(8,128)S(1)}, f32[2,56,128]{2,1,0:T(8,128)}, u32[]{:S(2)}) %copy-start) | copy-done | bytes 57368
  28.0 1.5 %copy-done.2 = bf16[1,256,3584]{2,1,0:T(8,128)(2,1)S(1)} copy-done((bf16[1,256,3584]{2,1,0:T(8,128)(2,1)S(1)}, bf16[1,256,3584]{2,1,0:T(8,128)(2,1)}, u32[]{:S(2)}) %copy-start.2) | copy-done | bytes 1835032
  29.5 1.1 %copy-done.3 = bf16[2,768,256]{2,1,0:T(8,128)(2,1)S(1)} copy-done((bf16[2,768,256]{2,1,0:T(8,128)(2,1)S(1)}, bf16[2,768,256]{2,1,0:T(8,128)(2,1)}, u32[]{:S(2)}) %copy-start.3) | copy-done | bytes 786456
  30.6 5.9 %shard_map.69 = f32[1,256,3584]{2,1,0:T(8,128)} custom-call(f32[1,256,3584]{2,1,0:T(8,128)S(1)} %copy-done.1, bf16[1,256,3584]{2,1,0:T(8,128)(2,1)S(1)} %copy-done.2, f32[2,56,128]{2,1,0:T(8,128)S(1)} %copy-done, bf16[2,768,256]{2,1,0:T(8,128)(2,1)S(1)} %copy-done.3), custom_call_target="tpu_custom_call" | custom-call | flops 8000000000 | bytes 28000000 | tf_op jit(solution)/shard_map/pallas_call | solution.py:220
  36.5 1.1 %collective-permute-done.6 = f32[2,2,56,128]{3,2,1,0:T(8,128)S(1)} collective-permute-done((f32[2,2,56,128]{3,2,1,0:T(8,128)S(1)}, f32[2,2,56,128]{3,2,1,0:T(8,128)S(1)}, u32[]{:S(2)}, u32[]{:S(2)}) %collective-permute-start.6) | collective-permute-done | bytes 114720 | tf_op jit(solution)/shard_map/ppermute | solution.py:173
  37.7 1.0 %collective-permute-start.9 = (f32[5,2,56,128]{3,2,1,0:T(8,128)S(1)}, f32[5,2,56,128]{3,2,1,0:T(8,128)S(1)}, u32[]{:S(2)}, u32[]{:S(2)}) collective-permute-start(f32[5,2,56,128]{3,2,1,0:T(8,128)S(1)} %constant_dynamic-update-slice_fusion.refs_4_.refs_7_), channel_id=1, source_target_pairs={{0,16},{8,24},{16,0},{24,8},{32,48},{40,56},{48,32},{56,40},{64,80... | collective-permute-start | bytes 860168 | tf_op jit(solution)/shard_map/ppermute | solution.py:173
  38.7 2.3 %collective-permute-start.8 = (f32[5,2,56,128]{3,2,1,0:T(8,128)S(1)}, f32[5,2,56,128]{3,2,1,0:T(8,128)S(1)}, u32[]{:S(2)}, u32[]{:S(2)}) collective-permute-start(f32[5,2,56,128]{3,2,1,0:T(8,128)S(1)} %constant_dynamic-update-slice_fusion.refs_4_.refs_7_), channel_id=1, source_target_pairs={{0,24},{8,0},{16,8},{24,16},{32,56},{40,32},{48,40},{56,48},{64,88... | collective-permute-start | bytes 860168 | tf_op jit(solution)/shard_map/ppermute | solution.py:173
  41.0 7.4 %shard_map.70.before_ref = f32[3584,256]{1,0:T(8,128)S(1)} custom-call(f32[3,2,56,128]{3,2,1,0:T(8,128)S(1)} %pad_maximum_fusion.refs_0_.refs_3_, f32[3,2,56,128]{3,2,1,0:T(8,128)S(1)} %collective-permute-done.2.refs_1_.refs_4_, f32[3,2,56,128]{3,2,1,0:T(8,128)S(1)} %collective-permute-done.3.refs_2_.refs_5_, ...), custom_call_target="tpu_custom_call" | custom-call | flops 7000000000 | bytes 24500000 | tf_op jit(solution)/shard_map/pallas_call | solution.py:234
  48.4 0.6 collective-permute-done.9.refs_2_
  49.0 3.3 %collective-permute-done.8.refs_1_ = f32[5,2,56,128]{3,2,1,0:T(8,128)S(1)} collective-permute-done((f32[5,2,56,128]{3,2,1,0:T(8,128)S(1)}, f32[5,2,56,128]{3,2,1,0:T(8,128)S(1)}, u32[]{:S(2)}, u32[]{:S(2)}) %collective-permute-start.8) | collective-permute-done | bytes 286752 | tf_op jit(solution)/shard_map/ppermute | solution.py:173
  52.4 0.3 collective-permute-done.7.refs_0_
  52.6 2.2 %shard_map.71 = (f32[15,2,56,128]{3,2,1,0:T(8,128)S(1)}, f32[8,128]{1,0:T(8,128)S(1)}) custom-call(f32[5,2,56,128]{3,2,1,0:T(8,128)S(1)} %collective-permute-done.7.refs_0_, f32[5,2,56,128]{3,2,1,0:T(8,128)S(1)} %collective-permute-done.8.refs_1_, f32[5,2,56,128]{3,2,1,0:T(8,128)S(1)} %collective-permute-done.9.refs_2_, ...), custom_call_target="tpu_custom_call" | custom-call | flops 2000000000 | bytes 7000000 | tf_op jit(solution)/shard_map/pallas_call | solution.py:245
  54.8 0.3 collective-permute-start.10
  55.1 1.2 %collective-permute-done.10 = f32[8,128]{1,0:T(8,128)S(1)} collective-permute-done((f32[8,128]{1,0:T(8,128)S(1)}, f32[8,128]{1,0:T(8,128)S(1)}, u32[]{:S(2)}, u32[]{:S(2)}) %collective-permute-start.10) | collective-permute-done | bytes 4128 | tf_op jit(solution)/shard_map/ppermute | solution.py:167
  56.2 3.2 %collective-permute-start.13 = (f32[8,128]{1,0:T(8,128)S(1)}, f32[8,128]{1,0:T(8,128)S(1)}, u32[]{:S(2)}, u32[]{:S(2)}) collective-permute-start(f32[8,128]{1,0:T(8,128)S(1)} %add.12), channel_id=1, source_target_pairs={{0,4},{1,5},{2,6},{3,7},{4,0},{5,1},{6,2},{7,3},{8,12},{9,13},{10,... | collective-permute-start | bytes 12296 | tf_op jit(solution)/shard_map/ppermute | solution.py:168
  59.4 1.1 %collective-permute-start.12 = (f32[8,128]{1,0:T(8,128)S(1)}, f32[8,128]{1,0:T(8,128)S(1)}, u32[]{:S(2)}, u32[]{:S(2)}) collective-permute-start(f32[8,128]{1,0:T(8,128)S(1)} %add.12), channel_id=1, source_target_pairs={{0,6},{1,7},{2,0},{3,1},{4,2},{5,3},{6,4},{7,5},{8,14},{9,15},{10,... | collective-permute-start | bytes 12296 | tf_op jit(solution)/shard_map/ppermute | solution.py:168
  60.5 1.0 %collective-permute-start.11 = (f32[8,128]{1,0:T(8,128)S(1)}, f32[8,128]{1,0:T(8,128)S(1)}, u32[]{:S(2)}, u32[]{:S(2)}) collective-permute-start(f32[8,128]{1,0:T(8,128)S(1)} %add.12), channel_id=1, source_target_pairs={{0,2},{1,3},{2,4},{3,5},{4,6},{5,7},{6,0},{7,1},{8,10},{9,11},{10,... | collective-permute-start | bytes 12296 | tf_op jit(solution)/shard_map/ppermute | solution.py:168
  61.5 7.4 %shard_map.72.x_ref = f32[256,3584]{1,0:T(8,128)S(1)} custom-call(f32[15,2,56,128]{3,2,1,0:T(8,128)S(1)} %get-tuple-element.22.p_ref, f32[3584,256]{1,0:T(8,128)S(1)} %shard_map.70.before_ref, bf16[2,768,256]{2,1,0:T(8,128)(2,1)S(1)} %copy-done.3), custom_call_target="tpu_custom_call" | custom-call | flops 8999999488 | bytes 31500000 | tf_op jit(solution)/shard_map/pallas_call | solution.py:255
  68.9 2.5 %shard_map.73 = f32[256,3584]{1,0:T(8,128)} custom-call(f32[256,3584]{1,0:T(8,128)S(1)} %shard_map.72.x_ref, f32[8,128]{1,0:T(8,128)S(1)} %add_add_fusion.total_ref), custom_call_target="tpu_custom_call" | custom-call | flops 2000000000 | bytes 7000000 | tf_op jit(solution)/shard_map/pallas_call | solution.py:266
  (19 shorter events, 0.1 us)
Async XLA Ops:
  2.2 24.9 %copy-start.1 = (f32[1,256,3584]{2,1,0:T(8,128)S(1)}, f32[1,256,3584]{2,1,0:T(8,128)}, u32[]{:S(2)}) copy-start(f32[1,256,3584]{2,1,0:T(8,128)} %m_ref.3) | copy-start | bytes 11010052
  8.9 4.4 %collective-permute-start = (f32[2,56,128]{2,1,0:T(8,128)}, f32[2,56,128]{2,1,0:T(8,128)S(1)}, u32[]{:S(2)}, u32[]{:S(2)}) collective-permute-start(f32[2,56,128]{2,1,0:T(8,128)} %shard_map.68.p_ref), channel_id=1, source_target_pairs={{0,32},{8,40},{16,48},{24,56},{32,64},{40,72},{48,80},{56,88},{64,... | collective-permute-start | bytes 172040 | tf_op jit(solution)/shard_map/ppermute | solution.py:173
  10.8 4.4 %collective-permute-start.1 = (f32[2,56,128]{2,1,0:T(8,128)}, f32[2,56,128]{2,1,0:T(8,128)S(1)}, u32[]{:S(2)}, u32[]{:S(2)}) collective-permute-start(f32[2,56,128]{2,1,0:T(8,128)} %shard_map.68.p_ref), channel_id=1, source_target_pairs={{0,224},{8,232},{16,240},{24,248},{32,0},{40,8},{48,16},{56,24},{6... | collective-permute-start | bytes 172040 | tf_op jit(solution)/shard_map/ppermute | solution.py:173
  16.0 21.6 %collective-permute-start.5 = (f32[3,2,56,128]{3,2,1,0:T(8,128)S(1)}, f32[3,2,56,128]{3,2,1,0:T(8,128)S(1)}, u32[]{:S(2)}, u32[]{:S(2)}) collective-permute-start(f32[3,2,56,128]{3,2,1,0:T(8,128)S(1)} %pad_maximum_fusion.refs_0_.refs_3_), channel_id=1, source_target_pairs={{0,96},{8,104},{16,112},{24,120},{32,128},{40,136},{48,144},{56,15... | collective-permute-start | bytes 516104 | tf_op jit(solution)/shard_map/ppermute | solution.py:173
  22.1 18.9 %collective-permute-start.4 = (f32[3,2,56,128]{3,2,1,0:T(8,128)S(1)}, f32[3,2,56,128]{3,2,1,0:T(8,128)S(1)}, u32[]{:S(2)}, u32[]{:S(2)}) collective-permute-start(f32[3,2,56,128]{3,2,1,0:T(8,128)S(1)} %pad_maximum_fusion.refs_0_.refs_3_), channel_id=1, source_target_pairs={{0,16},{8,24},{16,0},{24,8},{32,48},{40,56},{48,32},{56,40},{64,80... | collective-permute-start | bytes 516104 | tf_op jit(solution)/shard_map/ppermute | solution.py:173
  25.1 15.9 %collective-permute-start.3 = (f32[3,2,56,128]{3,2,1,0:T(8,128)S(1)}, f32[3,2,56,128]{3,2,1,0:T(8,128)S(1)}, u32[]{:S(2)}, u32[]{:S(2)}) collective-permute-start(f32[3,2,56,128]{3,2,1,0:T(8,128)S(1)} %pad_maximum_fusion.refs_0_.refs_3_), channel_id=1, source_target_pairs={{0,24},{8,0},{16,8},{24,16},{32,56},{40,32},{48,40},{56,48},{64,88... | collective-permute-start | bytes 516104 | tf_op jit(solution)/shard_map/ppermute | solution.py:173
  26.3 14.8 %collective-permute-start.2 = (f32[3,2,56,128]{3,2,1,0:T(8,128)S(1)}, f32[3,2,56,128]{3,2,1,0:T(8,128)S(1)}, u32[]{:S(2)}, u32[]{:S(2)}) collective-permute-start(f32[3,2,56,128]{3,2,1,0:T(8,128)S(1)} %pad_maximum_fusion.refs_0_.refs_3_), channel_id=1, source_target_pairs={{0,8},{8,16},{16,24},{24,0},{32,40},{40,48},{48,56},{56,32},{64,72... | collective-permute-start | bytes 516104 | tf_op jit(solution)/shard_map/ppermute | solution.py:173
  27.1 10.5 %collective-permute-start.6 = (f32[2,2,56,128]{3,2,1,0:T(8,128)S(1)}, f32[2,2,56,128]{3,2,1,0:T(8,128)S(1)}, u32[]{:S(2)}, u32[]{:S(2)}) collective-permute-start(f32[2,2,56,128]{3,2,1,0:T(8,128)S(1)} %pad_maximum_fusion.1), channel_id=1, source_target_pairs={{0,160},{8,168},{16,176},{24,184},{32,192},{40,200},{48,208},{56,2... | collective-permute-start | bytes 344072 | tf_op jit(solution)/shard_map/ppermute | solution.py:173
  27.1 0.8 %copy-start = (f32[2,56,128]{2,1,0:T(8,128)S(1)}, f32[2,56,128]{2,1,0:T(8,128)}, u32[]{:S(2)}) copy-start(f32[2,56,128]{2,1,0:T(8,128)} %shard_map.68.p_ref) | copy-start | bytes 172036
  28.0 1.5 %copy-start.2 = (bf16[1,256,3584]{2,1,0:T(8,128)(2,1)S(1)}, bf16[1,256,3584]{2,1,0:T(8,128)(2,1)}, u32[]{:S(2)}) copy-start(bf16[1,256,3584]{2,1,0:T(8,128)(2,1)} %g_ref.3) | copy-start | bytes 5505028
  29.5 1.1 %copy-start.3 = (bf16[2,768,256]{2,1,0:T(8,128)(2,1)S(1)}, bf16[2,768,256]{2,1,0:T(8,128)(2,1)}, u32[]{:S(2)}) copy-start(bf16[2,768,256]{2,1,0:T(8,128)(2,1)} %constant.7.clone.c_ref) | copy-start | bytes 2359300
  37.7 11.4 %collective-permute-start.9 = (f32[5,2,56,128]{3,2,1,0:T(8,128)S(1)}, f32[5,2,56,128]{3,2,1,0:T(8,128)S(1)}, u32[]{:S(2)}, u32[]{:S(2)}) collective-permute-start(f32[5,2,56,128]{3,2,1,0:T(8,128)S(1)} %constant_dynamic-update-slice_fusion.refs_4_.refs_7_), channel_id=1, source_target_pairs={{0,16},{8,24},{16,0},{24,8},{32,48},{40,56},{48,32},{56,40},{64,80... | collective-permute-start | bytes 860168 | tf_op jit(solution)/shard_map/ppermute | solution.py:173
  38.7 13.7 %collective-permute-start.8 = (f32[5,2,56,128]{3,2,1,0:T(8,128)S(1)}, f32[5,2,56,128]{3,2,1,0:T(8,128)S(1)}, u32[]{:S(2)}, u32[]{:S(2)}) collective-permute-start(f32[5,2,56,128]{3,2,1,0:T(8,128)S(1)} %constant_dynamic-update-slice_fusion.refs_4_.refs_7_), channel_id=1, source_target_pairs={{0,24},{8,0},{16,8},{24,16},{32,56},{40,32},{48,40},{56,48},{64,88... | collective-permute-start | bytes 860168 | tf_op jit(solution)/shard_map/ppermute | solution.py:173
  41.0 11.6 %collective-permute-start.7 = (f32[5,2,56,128]{3,2,1,0:T(8,128)S(1)}, f32[5,2,56,128]{3,2,1,0:T(8,128)S(1)}, u32[]{:S(2)}, u32[]{:S(2)}) collective-permute-start(f32[5,2,56,128]{3,2,1,0:T(8,128)S(1)} %constant_dynamic-update-slice_fusion.refs_4_.refs_7_), channel_id=1, source_target_pairs={{0,8},{8,16},{16,24},{24,0},{32,40},{40,48},{48,56},{56,32},{64,72... | collective-permute-start | bytes 860168 | tf_op jit(solution)/shard_map/ppermute | solution.py:173
  54.8 1.4 %collective-permute-start.10 = (f32[8,128]{1,0:T(8,128)S(1)}, f32[8,128]{1,0:T(8,128)S(1)}, u32[]{:S(2)}, u32[]{:S(2)}) collective-permute-start(f32[8,128]{1,0:T(8,128)S(1)} %get-tuple-element.24), channel_id=1, source_target_pairs={{0,1},{1,0},{2,3},{3,2},{4,5},{5,4},{6,7},{7,6},{8,9},{9,8},{10,11... | collective-permute-start | bytes 12296 | tf_op jit(solution)/shard_map/ppermute | solution.py:167
  56.2 12.7 %collective-permute-start.13 = (f32[8,128]{1,0:T(8,128)S(1)}, f32[8,128]{1,0:T(8,128)S(1)}, u32[]{:S(2)}, u32[]{:S(2)}) collective-permute-start(f32[8,128]{1,0:T(8,128)S(1)} %add.12), channel_id=1, source_target_pairs={{0,4},{1,5},{2,6},{3,7},{4,0},{5,1},{6,2},{7,3},{8,12},{9,13},{10,... | collective-permute-start | bytes 12296 | tf_op jit(solution)/shard_map/ppermute | solution.py:168
  59.4 9.5 %collective-permute-start.12 = (f32[8,128]{1,0:T(8,128)S(1)}, f32[8,128]{1,0:T(8,128)S(1)}, u32[]{:S(2)}, u32[]{:S(2)}) collective-permute-start(f32[8,128]{1,0:T(8,128)S(1)} %add.12), channel_id=1, source_target_pairs={{0,6},{1,7},{2,0},{3,1},{4,2},{5,3},{6,4},{7,5},{8,14},{9,15},{10,... | collective-permute-start | bytes 12296 | tf_op jit(solution)/shard_map/ppermute | solution.py:168
  60.5 8.4 %collective-permute-start.11 = (f32[8,128]{1,0:T(8,128)S(1)}, f32[8,128]{1,0:T(8,128)S(1)}, u32[]{:S(2)}, u32[]{:S(2)}) collective-permute-start(f32[8,128]{1,0:T(8,128)S(1)} %add.12), channel_id=1, source_target_pairs={{0,2},{1,3},{2,4},{3,5},{4,6},{5,7},{6,0},{7,1},{8,10},{9,11},{10,... | collective-permute-start | bytes 12296 | tf_op jit(solution)/shard_map/ppermute | solution.py:168
where the time goes:
time: 71.9 us; the launch traced here: 71.5 us
  Pallas kernels  32.1 us (45%)
  starting transfers between devices  22 us (31%)
  waiting for transfers between devices  9.92 us (14%)
  local copies, waits for them, and re-layouts  4.17 us (6%)
  other arithmetic  2.59 us (4%)
  between operations  0.74 us (1%)
    ppermute x10, starting transfers between devices, shift(): return lax.ppermute(x, 'dp', pairs)  16.5 us
    ppermute x10, waiting for transfers between devices, shift(): return lax.ppermute(x, 'dp', pairs)  8.76 us
    pallas_call x1, Pallas kernels, shards(): pl.pallas_call(late_kernel, grid=(steps,), in_specs=[whole(merged.shape),...  7.42 us
    pallas_call x1, Pallas kernels, shards(): pl.pallas_call(early_kernel, grid=(steps,), in_specs=[whole(x.shape) for...  7.39 us
    pallas_call x1, Pallas kernels, shards(): pl.pallas_call(values_kernel, grid=(steps,), in_specs=[field_spec, field_...  6.66 us
    pallas_call x1, Pallas kernels, shards(): pl.pallas_call(residual_kernel, grid=(steps,), in_specs=[field_spec, fiel...  5.92 us
    ppermute x3, starting transfers between devices, tensor_sum(): lax.ppermute(x, 'tensor', [(t, (t + k) % T) for t in range(T)])  5.22 us
    unnamed x9, local copies, waits for them, and re-layouts  3.47 us
  transfers between devices with their start and end apart: 14, of which 7 were waited for; matrix products, arithmetic and copies ran while one was open for 1% of the time, Pallas kernels for 29%

commit v1 on v0

--- a/solution.py
+++ b/solution.py
@@ -66,17 +66,22 @@
     return cells, cells + float(BLK)
 
 
-def values_kernel(m_ref, g_ref, e_ref, c_ref, p_ref):
+def values_kernel(m_ref, g_ref, k_ref, c_ref, p_ref):
     first = pl.program_id(0) * (WIDE // BLK)
     cells = cells_of()
+
+    @pl.when(pl.program_id(0) == 0)
+    def _():
+        band = lax.broadcasted_iota(jnp.int32, k_ref.shape, 0) % KEEP
+        p_ref[0] = (k_ref[...] - band * BAND).astype(jnp.float32).T
+
     for i in range(WIDE // TILE):
         coeffs = both_sides(field(m_ref, g_ref, i), c_ref)
         for q in range(4):
             row = pl.ds(first + i * 4 + q, 1)
-            e = e_ref[row, :]
+            e = p_ref[0, row, :]
             own = coeffs[block(q)]
             chosen = jnp.where(e == cells[0], own[:, :128], 0.0) + jnp.where(e == cells[1], own[:, 128:], 0.0)
-            p_ref[0, row, :] = e
             p_ref[1, row, :] = jnp.sum(chosen, axis=0, keepdims=True)
 
 
@@ -93,27 +98,39 @@
         o_ref[0, :, tile(i)] = field(m_ref, g_ref, i) - sent
 
 
-def merge_kernel(*refs, late):
-    *parts, p_ref, sq_ref = refs
-    held = replicas_of(parts)
-
-    def rows(g, squares):
-        at = pl.ds(pl.multiple_of(g * 8, 8), 8)
+def merge_kernel(*refs, groups, distinct, merged, squared):
+    outs = refs[sum(groups) :]
+    held, bounds = [], [0]
+    for count in groups:
+        start = len(bounds) - 1 and sum(groups[: len(bounds) - 1])
+        held += replicas_of(refs[start : start + count])
+        bounds.append(len(held))
+    group_of = [g for g in range(len(groups)) for _ in range(bounds[g], bounds[g + 1])]
+
+    def rows(step, squares):
+        at = pl.ds(pl.multiple_of(step * 8, 8), 8)
         places = [ref[r, 0, at, :] for ref, r in held]
         values = [ref[r, 1, at, :] for ref, r in held]
         for i in range(len(held)):
-            place, total = places[i], values[i]
-            for j in range(i + 1, len(held)):
-                if j == late:
-                    p_ref[i, 0, at, :] = place
-                    p_ref[i, 1, at, :] = total
+            place, total, group = places[i], values[i], group_of[i]
+            for j in range(i + 1, len(held) + 1):
+                if j == bounds[group + 1] and group < merged:
+                    outs[group][i - bounds[group], 0, at, :] = place
+                    outs[group][i - bounds[group], 1, at, :] = total
+                if j == len(held) or (not squared and group_of[j] != group):
+                    break
+                if distinct and group == len(groups) - 1:
+                    break
                 same = place == places[j]
                 total = total + jnp.where(same, values[j], 0.0)
                 places[j] = jnp.where(same, -1.0 - j, places[j])
-            squares = squares + jnp.where(place >= 0.0, total * total, 0.0)
+            if squared:
+                squares = squares + jnp.where(place >= 0.0, total * total, 0.0)
         return squares
 
-    sq_ref[...] = lax.fori_loop(0, p_ref.shape[2] // 8, rows, jnp.zeros((8, 128), jnp.float32))
+    squares = lax.fori_loop(0, refs[0].shape[2] // 8, rows, jnp.zeros((8, 128), jnp.float32))
+    if squared:
+        outs[-1][...] = squares
 
 
 def replicas_of(parts):
@@ -129,8 +146,9 @@
     return total
 
 
-def early_kernel(*refs):
+def add_kernel(*refs, distinct, before):
     *parts, s_ref = refs
+    before_ref = parts.pop() if before else None
     held = replicas_of(parts)
     first = pl.program_id(0) * (WIDE // BLK)
     cells = cells_of()
@@ -139,25 +157,39 @@
     def _(q):
         rows = pl.ds(pl.multiple_of(q * BLK, BLK), BLK)
         for half in range(2):
-            s_ref[rows, half * 128 : half * 128 + 128] = summed_row(held, pl.ds(first + q, 1), cells[half], False)
-
-
-def late_kernel(p_ref, before_ref, c_ref, o_ref):
+            lanes = slice(half * 128, half * 128 + 128)
+            total = summed_row(held, pl.ds(first + q, 1), cells[half], distinct)
+            s_ref[rows, lanes] = total + before_ref[rows, lanes] if before else total
+
+
+def late_tiles(p_ref, before_ref, c_ref, o_ref, first, scale):
     held = replicas_of([p_ref])
-    first = pl.program_id(0) * (WIDE // BLK)
     cells = cells_of()
     for i in range(WIDE // TILE):
         parts = []
         for q in range(4):
-            row = pl.ds(first + i * 4 + q, 1)
+            row = slice(first + i * 4 + q, first + i * 4 + q + 1)
             parts.append(jnp.concatenate([summed_row(held, row, cell, True) for cell in cells], axis=1))
         summed = before_ref[tile(i), :] + jnp.concatenate(parts, axis=0)
-        o_ref[:, tile(i)] = both_sides(summed, c_ref)
-
-
-def scale_kernel(x_ref, total_ref, o_ref):
+        out = both_sides(summed, c_ref)
+        o_ref[:, tile(i)] = out if scale is None else out * scale
+
+
+def left_kernel(p_ref, before_ref, c_ref, o_ref):
+    late_tiles(p_ref, before_ref, c_ref, o_ref, 0, None)
+
+
+def right_kernel(p_ref, before_ref, c_ref, x_ref, total_ref, o_ref):
     mean = jnp.sum(total_ref[...], keepdims=True) / (ROWS * FF)
-    o_ref[...] = x_ref[...] * lax.rsqrt(mean + epsilon)
+    scale = lax.rsqrt(mean + epsilon)
+
+    @pl.when(pl.program_id(0) == 0)
+    def _():
+        late_tiles(p_ref, before_ref, c_ref, o_ref, WIDE // BLK, scale)
+
+    @pl.when(pl.program_id(0) == 1)
+    def _():
+        o_ref[...] = x_ref[...] * scale
 
 
 Z, X, T = 8, 4, 8
@@ -174,7 +206,7 @@
 
 
 VMEM_LIMIT = 32 * 1024 * 1024
-MIDDLE = 44 * 1024 * 1024
+MIDDLE = 59 * 1024 * 1024
 BIG = 60 * 1024 * 1024
 
 
@@ -199,22 +231,21 @@
     width = momentum.shape[2]
     steps = width // WIDE
     blocks = width // BLK
-    band = jnp.arange(KEEP, dtype=jnp.int32) * BAND
-    offsets = jnp.transpose(kept[0] - band, (1, 0, 2)).reshape(blocks, 128).astype(jnp.float32)
     field_spec = pl.BlockSpec((1, ROWS, WIDE), lambda j: (0, 0, j))
     const_spec = whole(forward.shape)
+    places = jnp.transpose(kept[0], (0, 2, 1)).reshape(ROWS // BLK * KEEP, blocks)
     packet_spec = whole((2, blocks, 128))
     packet = pl.pallas_call(
         values_kernel,
         grid=(steps,),
-        in_specs=[field_spec, field_spec, whole((blocks, 128)), const_spec],
+        in_specs=[field_spec, field_spec, whole(places.shape), const_spec],
         out_specs=packet_spec,
         out_shape=jax.ShapeDtypeStruct((2, blocks, 128), jnp.float32),
         compiler_params=params(BIG),
         cost_estimate=cost(8),
-    )(momentum, gradient, offsets, forward)
+    )(momentum, gradient, places, forward)
     three = jnp.stack([shift(packet, 1, 0), packet, shift(packet, -1, 0)])
-    far = [shift(three, 3, 0), shift(three[:2], -3, 0)]
+    far = [shift(three, 3, 0), shift(three, -3, 0)]
     three_x = across(three)
     packet, three = lax.optimization_barrier((packet, three))
     residual = pl.pallas_call(
@@ -227,51 +258,64 @@
         cost_estimate=cost(8),
     )(momentum, gradient, packet, inverse)
     residual, *far = lax.optimization_barrier((residual, *far))
-    five = jnp.concatenate(far)
+    five = jnp.concatenate([far[0], far[1][:2]])
     five_x = across(five)
     sum_spec = pl.BlockSpec((WIDE, TILE), lambda j: (j, 0))
     early = [three, *three_x, five]
-    summed = pl.pallas_call(
-        early_kernel,
-        grid=(steps,),
-        in_specs=[whole(x.shape) for x in early],
-        out_specs=sum_spec,
-        out_shape=jax.ShapeDtypeStruct((width, TILE), jnp.float32),
+
+    def merge_call(groups, us, **flags):
+        parts = [x for group in groups for x in group]
+        shapes = [
+            jax.ShapeDtypeStruct((sum(x.shape[0] for x in group), 2, blocks, 128), jnp.float32)
+            for group in groups[: flags["merged"]]
+        ]
+        if flags["squared"]:
+            shapes.append(jax.ShapeDtypeStruct((8, 128), jnp.float32))
+        return pl.pallas_call(
+            functools.partial(merge_kernel, groups=[len(group) for group in groups], **flags),
+            out_shape=shapes,
+            compiler_params=params(),
+            cost_estimate=cost(us),
+        )(*parts)
+
+    def add_call(parts, before, distinct, us):
+        return pl.pallas_call(
+            functools.partial(add_kernel, distinct=distinct, before=len(before) > 0),
+            grid=(steps,),
+            in_specs=[whole(x.shape) for x in parts] + [sum_spec] * len(before),
+            out_specs=sum_spec,
+            out_shape=jax.ShapeDtypeStruct((width, TILE), jnp.float32),
+            input_output_aliases={len(parts): 0} if before else {},
+            compiler_params=params(),
+            cost_estimate=cost(us),
+        )(*parts, *before)
+
+    (early_merged,) = merge_call([early], 1, distinct=False, merged=1, squared=False)
+    summed = add_call([early_merged], [], True, 5)
+    summed, *five_x = lax.optimization_barrier((summed, *five_x))
+    merged, squares = merge_call([five_x, [early_merged]], 2, distinct=True, merged=1, squared=True)
+    total = tensor_sum(squares)
+    half_shape = jax.ShapeDtypeStruct((ROWS, WIDE), jnp.float32)
+    half_spec = whole(half_shape.shape)
+    combined = pl.pallas_call(
+        left_kernel,
+        grid=(1,),
+        in_specs=[whole(merged.shape), pl.BlockSpec((WIDE, TILE), lambda j: (0, 0)), const_spec],
+        out_specs=half_spec,
+        out_shape=half_shape,
         compiler_params=params(),
-        cost_estimate=cost(7),
-    )(*early)
-    summed, *five_x = lax.optimization_barrier((summed, *five_x))
-    late = sum(x.shape[0] for x in five_x)
-    merged, squares = pl.pallas_call(
-        functools.partial(merge_kernel, late=late),
-        out_shape=(
-            jax.ShapeDtypeStruct((late, 2, blocks, 128), jnp.float32),
-            jax.ShapeDtypeStruct((8, 128), jnp.float32),
-        ),
-        compiler_params=params(),
-        cost_estimate=cost(2),
-    )(*five_x, *early)
-    total = tensor_sum(squares)
-    combined = pl.pallas_call(
-        late_kernel,
-        grid=(steps,),
-        in_specs=[whole(merged.shape), sum_spec, const_spec],
-        out_specs=pl.BlockSpec((ROWS, WIDE), lambda j: (0, j)),
+        cost_estimate=cost(4),
+    )(merged, summed, inverse)
+    combined, total = lax.optimization_barrier((combined, total))
+    update = pl.pallas_call(
+        right_kernel,
+        grid=(2,),
+        in_specs=[whole(merged.shape), pl.BlockSpec((WIDE, TILE), lambda j: (1, 0)), const_spec, half_spec, whole((8, 128))],
+        out_specs=pl.BlockSpec((ROWS, WIDE), lambda j: (0, 1 - j)),
         out_shape=jax.ShapeDtypeStruct((ROWS, width), jnp.float32),
         compiler_params=params(),
-        cost_estimate=cost(9),
-    )(merged, summed, inverse)
-    combined, total = lax.optimization_barrier((combined, total))
-    scale_spec = pl.BlockSpec((64, width), lambda j: (j, 0))
-    update = pl.pallas_call(
-        scale_kernel,
-        grid=(ROWS // 64,),
-        in_specs=[scale_spec, whole((8, 128))],
-        out_specs=scale_spec,
-        out_shape=jax.ShapeDtypeStruct((ROWS, width), jnp.float32),
-        compiler_params=params(),
-        cost_estimate=cost(2),
-    )(combined, total)
+        cost_estimate=cost(5),
+    )(merged, summed, inverse, combined, total)
     return (update, residual)
 
 

time: 71.9 us -> 68 us (0.946)
  waiting for transfers between devices: 9.92 us -> 14.3 us
  local copies, waits for them, and re-layouts: 4.17 us -> 0.02 us
  Pallas kernels: 32.1 us -> 29.4 us
  other arithmetic: 2.59 us -> 0.87 us
    ppermute x10, waiting for transfers between devices: 8.76 us -> 12.8 us  [shift(): return lax.ppermute(x, 'dp', pairs)]
    pallas_call x4 -> x5, Pallas kernels: 19.5 us -> 15.6 us  [the longest x1 5.46 us: shards(): pl.pallas_call(right_kernel, grid=(2,), in_specs=[whole(merged.shape), pl...]
    unnamed x9 -> x2, local copies, waits for them, and re-layouts: 3.47 us -> 0.01 us
    pallas_call x1, Pallas kernels: 5.92 us -> 7.16 us  [shards(): pl.pallas_call(residual_kernel, grid=(steps,), in_specs=[field_spec, fiel...]
    convert_element_type x1 -> x0, other arithmetic: 0.92 us -> none  [shards(): jnp.transpose(kept[0] - band, (1, 0, 2)).reshape(blocks, 128)]
    ppermute x10, starting transfers between devices: 16.5 us -> 17.3 us  [shift(): return lax.ppermute(x, 'dp', pairs)]
    another operation x2 -> x1, other arithmetic: 1.66 us -> 0.83 us  [shards(): three = jnp.stack([shift(packet, 1, 0), packet, shift(packet, -1, 0)])]
  transfers between devices with their start and end apart: 14 -> 14, of which waited for: 7 -> 7; matrix products, arithmetic and copies ran while one was open for 1% -> 0% of each run, Pallas kernels for 29% -> 23%
where the time goes in v1:
time: 68 us; the launch traced here: 67.9 us
  Pallas kernels  29.4 us (43%)
  starting transfers between devices  22.6 us (33%)
  waiting for transfers between devices  14.3 us (21%)
  other arithmetic  0.87 us (1%)
  between operations  0.71 us (1%)
    ppermute x10, starting transfers between devices, shift(): return lax.ppermute(x, 'dp', pairs)  17.3 us
    ppermute x10, waiting for transfers between devices, shift(): return lax.ppermute(x, 'dp', pairs)  12.8 us
    pallas_call x1, Pallas kernels, shards(): pl.pallas_call(residual_kernel, grid=(steps,), in_specs=[field_spec, fiel...  7.16 us
    pallas_call x1, Pallas kernels, shards(): pl.pallas_call(values_kernel, grid=(steps,), in_specs=[field_spec, field_...  6.62 us
    pallas_call x1, Pallas kernels, shards(): pl.pallas_call(right_kernel, grid=(2,), in_specs=[whole(merged.shape), pl...  5.46 us
    ppermute x3, starting transfers between devices, tensor_sum(): lax.ppermute(x, 'tensor', [(t, (t + k) % T) for t in range(T)])  5.22 us
    pallas_call x1, Pallas kernels, add_call(): pl.pallas_call(functools.partial(add_kernel, distinct=distinct, before=le...  4.41 us
    pallas_call x1, Pallas kernels, shards(): pl.pallas_call(left_kernel, grid=(1,), in_specs=[whole(merged.shape), pl....  3.45 us
  transfers between devices with their start and end apart: 14, of which 7 were waited for; matrix products, arithmetic and copies ran while one was open for 0% of the time, Pallas kernels for 23%

profile of v1, /device:TPU:32, one launch (start us, length us, event | category | flops | bytes accessed | tf_op | source)
XLA Modules:
  0.0 67.9 jit_solution(12717815221811038619)
XLA Ops:
  0.6 6.6 %shard_map.68.p_ref = f32[2,56,128]{2,1,0:T(8,128)} custom-call(f32[1,256,3584]{2,1,0:T(8,128)} %m_ref.3, bf16[1,256,3584]{2,1,0:T(8,128)(2,1)} %g_ref.3, s32[128,56]{1,0:T(8,128)} %bitcast.11, bf16[2,768,256]{2,1,0:T(8,128)(2,1)} %constant.4.clone.c_ref), custom_call_target="tpu_custom_call" | custom-call | flops 8000000000 | bytes 28000000 | tf_op jit(solution)/shard_map/pallas_call | solution.py:238
  7.2 1.8 %collective-permute-start.1 = (f32[2,56,128]{2,1,0:T(8,128)}, f32[2,56,128]{2,1,0:T(8,128)S(1)}, u32[]{:S(2)}, u32[]{:S(2)}) collective-permute-start(f32[2,56,128]{2,1,0:T(8,128)} %shard_map.68.p_ref), channel_id=1, source_target_pairs={{0,224},{8,232},{16,240},{24,248},{32,0},{40,8},{48,16},{56,24},{6... | collective-permute-start | bytes 172040 | tf_op jit(solution)/shard_map/ppermute | solution.py:205
  9.1 0.2 collective-permute-start
  9.3 2.4 %collective-permute-done.1 = f32[2,56,128]{2,1,0:T(8,128)S(1)} collective-permute-done((f32[2,56,128]{2,1,0:T(8,128)}, f32[2,56,128]{2,1,0:T(8,128)S(1)}, u32[]{:S(2)}, u32[]{:S(2)}) %collective-permute-start.1) | collective-permute-done | bytes 57376 | tf_op jit(solution)/shard_map/ppermute | solution.py:205
  11.6 4.0 %collective-permute-done = f32[2,56,128]{2,1,0:T(8,128)S(1)} collective-permute-done((f32[2,56,128]{2,1,0:T(8,128)}, f32[2,56,128]{2,1,0:T(8,128)S(1)}, u32[]{:S(2)}, u32[]{:S(2)}) %collective-permute-start) | collective-permute-done | bytes 57376 | tf_op jit(solution)/shard_map/ppermute | solution.py:205
  15.6 0.8 %pad_maximum_fusion.1.refs_0_ = f32[3,2,56,128]{3,2,1,0:T(8,128)S(1)} fusion(f32[1,2,56,128]{3,2,1,0:T(8,128)S(1)} %bitcast.9, f32[1,2,56,128]{3,2,1,0:T(8,128)} %bitcast.8, f32[1,2,56,128]{3,2,1,0:T(8,128)S(1)} %bitcast.10), kind=kLoop, calls=%fused_computation.1 | loop fusion | flops 86016 | bytes 344064 | tf_op jit(solution)/shard_map/stack | solution.py:247
  16.4 3.0 %collective-permute-start.6 = (f32[3,2,56,128]{3,2,1,0:T(8,128)S(1)}, f32[3,2,56,128]{3,2,1,0:T(8,128)S(1)}, u32[]{:S(2)}, u32[]{:S(2)}) collective-permute-start(f32[3,2,56,128]{3,2,1,0:T(8,128)S(1)} %pad_maximum_fusion.1.refs_0_), channel_id=1, source_target_pairs={{0,160},{8,168},{16,176},{24,184},{32,192},{40,200},{48,208},{56,2... | collective-permute-start | bytes 516104 | tf_op jit(solution)/shard_map/ppermute | solution.py:205
  19.4 2.2 %collective-permute-start.5 = (f32[3,2,56,128]{3,2,1,0:T(8,128)S(1)}, f32[3,2,56,128]{3,2,1,0:T(8,128)S(1)}, u32[]{:S(2)}, u32[]{:S(2)}) collective-permute-start(f32[3,2,56,128]{3,2,1,0:T(8,128)S(1)} %pad_maximum_fusion.1.refs_0_), channel_id=1, source_target_pairs={{0,96},{8,104},{16,112},{24,120},{32,128},{40,136},{48,144},{56,15... | collective-permute-start | bytes 516104 | tf_op jit(solution)/shard_map/ppermute | solution.py:205
  21.6 3.0 %collective-permute-start.4 = (f32[3,2,56,128]{3,2,1,0:T(8,128)S(1)}, f32[3,2,56,128]{3,2,1,0:T(8,128)S(1)}, u32[]{:S(2)}, u32[]{:S(2)}) collective-permute-start(f32[3,2,56,128]{3,2,1,0:T(8,128)S(1)} %pad_maximum_fusion.1.refs_0_), channel_id=1, source_target_pairs={{0,16},{8,24},{16,0},{24,8},{32,48},{40,56},{48,32},{56,40},{64,80... | collective-permute-start | bytes 516104 | tf_op jit(solution)/shard_map/ppermute | solution.py:205
  24.6 1.1 %collective-permute-start.3 = (f32[3,2,56,128]{3,2,1,0:T(8,128)S(1)}, f32[3,2,56,128]{3,2,1,0:T(8,128)S(1)}, u32[]{:S(2)}, u32[]{:S(2)}) collective-permute-start(f32[3,2,56,128]{3,2,1,0:T(8,128)S(1)} %pad_maximum_fusion.1.refs_0_), channel_id=1, source_target_pairs={{0,24},{8,0},{16,8},{24,16},{32,56},{40,32},{48,40},{56,48},{64,88... | collective-permute-start | bytes 516104 | tf_op jit(solution)/shard_map/ppermute | solution.py:205
  25.7 0.9 %collective-permute-start.2 = (f32[3,2,56,128]{3,2,1,0:T(8,128)S(1)}, f32[3,2,56,128]{3,2,1,0:T(8,128)S(1)}, u32[]{:S(2)}, u32[]{:S(2)}) collective-permute-start(f32[3,2,56,128]{3,2,1,0:T(8,128)S(1)} %pad_maximum_fusion.1.refs_0_), channel_id=1, source_target_pairs={{0,8},{8,16},{16,24},{24,0},{32,40},{40,48},{48,56},{56,32},{64,72... | collective-permute-start | bytes 516104 | tf_op jit(solution)/shard_map/ppermute | solution.py:205
  26.6 7.2 %shard_map.69 = f32[1,256,3584]{2,1,0:T(8,128)} custom-call(f32[1,256,3584]{2,1,0:T(8,128)} %m_ref.3, bf16[1,256,3584]{2,1,0:T(8,128)(2,1)} %g_ref.3, f32[2,56,128]{2,1,0:T(8,128)} %shard_map.68.p_ref, bf16[2,768,256]{2,1,0:T(8,128)(2,1)} %constant.5.clone.c_ref), custom_call_target="tpu_custom_call" | custom-call | flops 8000000000 | bytes 28000000 | tf_op jit(solution)/shard_map/pallas_call | solution.py:251
  33.8 0.0 collective-permute-done.6
  33.8 0.1 collective-permute-done.5
  33.9 3.1 %collective-permute-start.9 = (f32[5,2,56,128]{3,2,1,0:T(8,128)S(1)}, f32[5,2,56,128]{3,2,1,0:T(8,128)S(1)}, u32[]{:S(2)}, u32[]{:S(2)}) collective-permute-start(f32[5,2,56,128]{3,2,1,0:T(8,128)S(1)} %pad_maximum_fusion.refs_4_), channel_id=1, source_target_pairs={{0,16},{8,24},{16,0},{24,8},{32,48},{40,56},{48,32},{56,40},{64,80... | collective-permute-start | bytes 860168 | tf_op jit(solution)/shard_map/ppermute | solution.py:205
  37.0 1.1 %collective-permute-start.8 = (f32[5,2,56,128]{3,2,1,0:T(8,128)S(1)}, f32[5,2,56,128]{3,2,1,0:T(8,128)S(1)}, u32[]{:S(2)}, u32[]{:S(2)}) collective-permute-start(f32[5,2,56,128]{3,2,1,0:T(8,128)S(1)} %pad_maximum_fusion.refs_4_), channel_id=1, source_target_pairs={{0,24},{8,0},{16,8},{24,16},{32,56},{40,32},{48,40},{56,48},{64,88... | collective-permute-start | bytes 860168 | tf_op jit(solution)/shard_map/ppermute | solution.py:205
  38.1 0.0 collective-permute-done.4.refs_3_
  38.1 0.9 %collective-permute-start.7 = (f32[5,2,56,128]{3,2,1,0:T(8,128)S(1)}, f32[5,2,56,128]{3,2,1,0:T(8,128)S(1)}, u32[]{:S(2)}, u32[]{:S(2)}) collective-permute-start(f32[5,2,56,128]{3,2,1,0:T(8,128)S(1)} %pad_maximum_fusion.refs_4_), channel_id=1, source_target_pairs={{0,8},{8,16},{16,24},{24,0},{32,40},{40,48},{48,56},{56,32},{64,72... | collective-permute-start | bytes 860168 | tf_op jit(solution)/shard_map/ppermute | solution.py:205
  39.0 0.5 shard_map.70.refs_0_.refs_3_
  39.6 4.4 %shard_map.71.before_ref = f32[3584,256]{1,0:T(8,128)S(1)} custom-call(f32[17,2,56,128]{3,2,1,0:T(8,128)S(1)} %shard_map.70.refs_0_.refs_3_), custom_call_target="tpu_custom_call" | custom-call | flops 5000000000 | bytes 17500000 | tf_op jit(solution)/shard_map/pallas_call | solution.py:282
  44.0 0.0 copy-start
  44.0 1.2 %collective-permute-done.9.refs_2_ = f32[5,2,56,128]{3,2,1,0:T(8,128)S(1)} collective-permute-done((f32[5,2,56,128]{3,2,1,0:T(8,128)S(1)}, f32[5,2,56,128]{3,2,1,0:T(8,128)S(1)}, u32[]{:S(2)}, u32[]{:S(2)}) %collective-permute-start.9) | collective-permute-done | bytes 286752 | tf_op jit(solution)/shard_map/ppermute | solution.py:205
  45.2 5.2 %collective-permute-done.8.refs_1_ = f32[5,2,56,128]{3,2,1,0:T(8,128)S(1)} collective-permute-done((f32[5,2,56,128]{3,2,1,0:T(8,128)S(1)}, f32[5,2,56,128]{3,2,1,0:T(8,128)S(1)}, u32[]{:S(2)}, u32[]{:S(2)}) %collective-permute-start.8) | collective-permute-done | bytes 286752 | tf_op jit(solution)/shard_map/ppermute | solution.py:205
  50.4 1.7 %shard_map.72 = (f32[15,2,56,128]{3,2,1,0:T(8,128)S(1)}, f32[8,128]{1,0:T(8,128)S(1)}) custom-call(f32[5,2,56,128]{3,2,1,0:T(8,128)S(1)} %collective-permute-done.7.refs_0_, f32[5,2,56,128]{3,2,1,0:T(8,128)S(1)} %collective-permute-done.8.refs_1_, f32[5,2,56,128]{3,2,1,0:T(8,128)S(1)} %collective-permute-done.9.refs_2_, ...), custom_call_target="tpu_custom_call" | custom-call | flops 2000000000 | bytes 7000000 | tf_op jit(solution)/shard_map/pallas_call | solution.py:274
  52.1 0.1 collective-permute-start.10
  52.2 1.2 %collective-permute-done.10 = f32[8,128]{1,0:T(8,128)S(1)} collective-permute-done((f32[8,128]{1,0:T(8,128)S(1)}, f32[8,128]{1,0:T(8,128)S(1)}, u32[]{:S(2)}, u32[]{:S(2)}) %collective-permute-start.10) | collective-permute-done | bytes 4128 | tf_op jit(solution)/shard_map/ppermute | solution.py:199
  53.4 3.2 %collective-permute-start.13 = (f32[8,128]{1,0:T(8,128)S(1)}, f32[8,128]{1,0:T(8,128)S(1)}, u32[]{:S(2)}, u32[]{:S(2)}) collective-permute-start(f32[8,128]{1,0:T(8,128)S(1)} %add.12), channel_id=1, source_target_pairs={{0,4},{1,5},{2,6},{3,7},{4,0},{5,1},{6,2},{7,3},{8,12},{9,13},{10,... | collective-permute-start | bytes 12296 | tf_op jit(solution)/shard_map/ppermute | solution.py:200
  56.6 1.1 %collective-permute-start.12 = (f32[8,128]{1,0:T(8,128)S(1)}, f32[8,128]{1,0:T(8,128)S(1)}, u32[]{:S(2)}, u32[]{:S(2)}) collective-permute-start(f32[8,128]{1,0:T(8,128)S(1)} %add.12), channel_id=1, source_target_pairs={{0,6},{1,7},{2,0},{3,1},{4,2},{5,3},{6,4},{7,5},{8,14},{9,15},{10,... | collective-permute-start | bytes 12296 | tf_op jit(solution)/shard_map/ppermute | solution.py:200
  57.6 1.0 %collective-permute-start.11 = (f32[8,128]{1,0:T(8,128)S(1)}, f32[8,128]{1,0:T(8,128)S(1)}, u32[]{:S(2)}, u32[]{:S(2)}) collective-permute-start(f32[8,128]{1,0:T(8,128)S(1)} %add.12), channel_id=1, source_target_pairs={{0,2},{1,3},{2,4},{3,5},{4,6},{5,7},{6,0},{7,1},{8,10},{9,11},{10,... | collective-permute-start | bytes 12296 | tf_op jit(solution)/shard_map/ppermute | solution.py:200
  58.6 3.4 %shard_map.73.x_ref = f32[256,1792]{1,0:T(8,128)S(1)} custom-call(f32[15,2,56,128]{3,2,1,0:T(8,128)S(1)} %get-tuple-element.22.p_ref, f32[3584,256]{1,0:T(8,128)S(1)} %shard_map.71.before_ref, bf16[2,768,256]{2,1,0:T(8,128)(2,1)S(1)} %copy-done), custom_call_target="tpu_custom_call" | custom-call | flops 4000000000 | bytes 14000000 | tf_op jit(solution)/shard_map/pallas_call | solution.py:300
  62.1 0.4 collective-permute-done.11
  62.4 5.5 %shard_map.74 = f32[256,3584]{1,0:T(8,128)} custom-call(f32[15,2,56,128]{3,2,1,0:T(8,128)S(1)} %get-tuple-element.22.p_ref, f32[3584,256]{1,0:T(8,128)S(1)} %shard_map.71.before_ref, bf16[2,768,256]{2,1,0:T(8,128)(2,1)S(1)} %copy-done, f32[256,1792]{1,0:T(8,128)S(1)} %shard_map.73.x_ref, f32[8,128]{1,0:T(8,128)S(1)} %add_add_fusion.total_ref), custom_call_target="tpu_custom_call" | custom-call | flops 5000000000 | bytes 17500000 | tf_op jit(solution)/shard_map/pallas_call | solution.py:310
  (10 shorter events, 0.1 us)
Async XLA Ops:
  7.2 4.4 %collective-permute-start.1 = (f32[2,56,128]{2,1,0:T(8,128)}, f32[2,56,128]{2,1,0:T(8,128)S(1)}, u32[]{:S(2)}, u32[]{:S(2)}) collective-permute-start(f32[2,56,128]{2,1,0:T(8,128)} %shard_map.68.p_ref), channel_id=1, source_target_pairs={{0,224},{8,232},{16,240},{24,248},{32,0},{40,8},{48,16},{56,24},{6... | collective-permute-start | bytes 172040 | tf_op jit(solution)/shard_map/ppermute | solution.py:205
  9.1 6.5 %collective-permute-start = (f32[2,56,128]{2,1,0:T(8,128)}, f32[2,56,128]{2,1,0:T(8,128)S(1)}, u32[]{:S(2)}, u32[]{:S(2)}) collective-permute-start(f32[2,56,128]{2,1,0:T(8,128)} %shard_map.68.p_ref), channel_id=1, source_target_pairs={{0,32},{8,40},{16,48},{24,56},{32,64},{40,72},{48,80},{56,88},{64,... | collective-permute-start | bytes 172040 | tf_op jit(solution)/shard_map/ppermute | solution.py:205
  16.4 17.3 %collective-permute-start.6 = (f32[3,2,56,128]{3,2,1,0:T(8,128)S(1)}, f32[3,2,56,128]{3,2,1,0:T(8,128)S(1)}, u32[]{:S(2)}, u32[]{:S(2)}) collective-permute-start(f32[3,2,56,128]{3,2,1,0:T(8,128)S(1)} %pad_maximum_fusion.1.refs_0_), channel_id=1, source_target_pairs={{0,160},{8,168},{16,176},{24,184},{32,192},{40,200},{48,208},{56,2... | collective-permute-start | bytes 516104 | tf_op jit(solution)/shard_map/ppermute | solution.py:205
  19.4 14.4 %collective-permute-start.5 = (f32[3,2,56,128]{3,2,1,0:T(8,128)S(1)}, f32[3,2,56,128]{3,2,1,0:T(8,128)S(1)}, u32[]{:S(2)}, u32[]{:S(2)}) collective-permute-start(f32[3,2,56,128]{3,2,1,0:T(8,128)S(1)} %pad_maximum_fusion.1.refs_0_), channel_id=1, source_target_pairs={{0,96},{8,104},{16,112},{24,120},{32,128},{40,136},{48,144},{56,15... | collective-permute-start | bytes 516104 | tf_op jit(solution)/shard_map/ppermute | solution.py:205
  21.6 16.6 %collective-permute-start.4 = (f32[3,2,56,128]{3,2,1,0:T(8,128)S(1)}, f32[3,2,56,128]{3,2,1,0:T(8,128)S(1)}, u32[]{:S(2)}, u32[]{:S(2)}) collective-permute-start(f32[3,2,56,128]{3,2,1,0:T(8,128)S(1)} %pad_maximum_fusion.1.refs_0_), channel_id=1, source_target_pairs={{0,16},{8,24},{16,0},{24,8},{32,48},{40,56},{48,32},{56,40},{64,80... | collective-permute-start | bytes 516104 | tf_op jit(solution)/shard_map/ppermute | solution.py:205
  24.6 14.4 %collective-permute-start.3 = (f32[3,2,56,128]{3,2,1,0:T(8,128)S(1)}, f32[3,2,56,128]{3,2,1,0:T(8,128)S(1)}, u32[]{:S(2)}, u32[]{:S(2)}) collective-permute-start(f32[3,2,56,128]{3,2,1,0:T(8,128)S(1)} %pad_maximum_fusion.1.refs_0_), channel_id=1, source_target_pairs={{0,24},{8,0},{16,8},{24,16},{32,56},{40,32},{48,40},{56,48},{64,88... | collective-permute-start | bytes 516104 | tf_op jit(solution)/shard_map/ppermute | solution.py:205
  25.7 13.3 %collective-permute-start.2 = (f32[3,2,56,128]{3,2,1,0:T(8,128)S(1)}, f32[3,2,56,128]{3,2,1,0:T(8,128)S(1)}, u32[]{:S(2)}, u32[]{:S(2)}) collective-permute-start(f32[3,2,56,128]{3,2,1,0:T(8,128)S(1)} %pad_maximum_fusion.1.refs_0_), channel_id=1, source_target_pairs={{0,8},{8,16},{16,24},{24,0},{32,40},{40,48},{48,56},{56,32},{64,72... | collective-permute-start | bytes 516104 | tf_op jit(solution)/shard_map/ppermute | solution.py:205
  33.9 11.3 %collective-permute-start.9 = (f32[5,2,56,128]{3,2,1,0:T(8,128)S(1)}, f32[5,2,56,128]{3,2,1,0:T(8,128)S(1)}, u32[]{:S(2)}, u32[]{:S(2)}) collective-permute-start(f32[5,2,56,128]{3,2,1,0:T(8,128)S(1)} %pad_maximum_fusion.refs_4_), channel_id=1, source_target_pairs={{0,16},{8,24},{16,0},{24,8},{32,48},{40,56},{48,32},{56,40},{64,80... | collective-permute-start | bytes 860168 | tf_op jit(solution)/shard_map/ppermute | solution.py:205
  37.0 13.4 %collective-permute-start.8 = (f32[5,2,56,128]{3,2,1,0:T(8,128)S(1)}, f32[5,2,56,128]{3,2,1,0:T(8,128)S(1)}, u32[]{:S(2)}, u32[]{:S(2)}) collective-permute-start(f32[5,2,56,128]{3,2,1,0:T(8,128)S(1)} %pad_maximum_fusion.refs_4_), channel_id=1, source_target_pairs={{0,24},{8,0},{16,8},{24,16},{32,56},{40,32},{48,40},{56,48},{64,88... | collective-permute-start | bytes 860168 | tf_op jit(solution)/shard_map/ppermute | solution.py:205
  38.1 12.3 %collective-permute-start.7 = (f32[5,2,56,128]{3,2,1,0:T(8,128)S(1)}, f32[5,2,56,128]{3,2,1,0:T(8,128)S(1)}, u32[]{:S(2)}, u32[]{:S(2)}) collective-permute-start(f32[5,2,56,128]{3,2,1,0:T(8,128)S(1)} %pad_maximum_fusion.refs_4_), channel_id=1, source_target_pairs={{0,8},{8,16},{16,24},{24,0},{32,40},{40,48},{48,56},{56,32},{64,72... | collective-permute-start | bytes 860168 | tf_op jit(solution)/shard_map/ppermute | solution.py:205
  44.0 14.6 %copy-start = (bf16[2,768,256]{2,1,0:T(8,128)(2,1)S(1)}, bf16[2,768,256]{2,1,0:T(8,128)(2,1)}, u32[]{:S(2)}) copy-start(bf16[2,768,256]{2,1,0:T(8,128)(2,1)} %constant.5.clone.c_ref) | copy-start | bytes 2359300
  52.1 1.2 %collective-permute-start.10 = (f32[8,128]{1,0:T(8,128)S(1)}, f32[8,128]{1,0:T(8,128)S(1)}, u32[]{:S(2)}, u32[]{:S(2)}) collective-permute-start(f32[8,128]{1,0:T(8,128)S(1)} %get-tuple-element.24), channel_id=1, source_target_pairs={{0,1},{1,0},{2,3},{3,2},{4,5},{5,4},{6,7},{7,6},{8,9},{9,8},{10,11... | collective-permute-start | bytes 12296 | tf_op jit(solution)/shard_map/ppermute | solution.py:199
  53.4 8.7 %collective-permute-start.13 = (f32[8,128]{1,0:T(8,128)S(1)}, f32[8,128]{1,0:T(8,128)S(1)}, u32[]{:S(2)}, u32[]{:S(2)}) collective-permute-start(f32[8,128]{1,0:T(8,128)S(1)} %add.12), channel_id=1, source_target_pairs={{0,4},{1,5},{2,6},{3,7},{4,0},{5,1},{6,2},{7,3},{8,12},{9,13},{10,... | collective-permute-start | bytes 12296 | tf_op jit(solution)/shard_map/ppermute | solution.py:200
  56.6 5.5 %collective-permute-start.12 = (f32[8,128]{1,0:T(8,128)S(1)}, f32[8,128]{1,0:T(8,128)S(1)}, u32[]{:S(2)}, u32[]{:S(2)}) collective-permute-start(f32[8,128]{1,0:T(8,128)S(1)} %add.12), channel_id=1, source_target_pairs={{0,6},{1,7},{2,0},{3,1},{4,2},{5,3},{6,4},{7,5},{8,14},{9,15},{10,... | collective-permute-start | bytes 12296 | tf_op jit(solution)/shard_map/ppermute | solution.py:200
  57.6 4.8 %collective-permute-start.11 = (f32[8,128]{1,0:T(8,128)S(1)}, f32[8,128]{1,0:T(8,128)S(1)}, u32[]{:S(2)}, u32[]{:S(2)}) collective-permute-start(f32[8,128]{1,0:T(8,128)S(1)} %add.12), channel_id=1, source_target_pairs={{0,2},{1,3},{2,4},{3,5},{4,6},{5,7},{6,0},{7,1},{8,10},{9,11},{10,... | collective-permute-start | bytes 12296 | tf_op jit(solution)/shard_map/ppermute | solution.py:200

commit v2 on v1

--- a/solution.py
+++ b/solution.py
@@ -85,13 +85,13 @@
             p_ref[1, row, :] = jnp.sum(chosen, axis=0, keepdims=True)
 
 
-def residual_kernel(m_ref, g_ref, p_ref, c_ref, o_ref):
-    first = pl.program_id(0) * (WIDE // BLK)
+def residual_kernel(m_ref, g_ref, p_ref, c_ref, *rest, first):
+    o_ref = rest[-1]
     cells = cells_of()
     for i in range(WIDE // TILE):
         parts = []
         for q in range(4):
-            row = pl.ds(first + i * 4 + q, 1)
+            row = slice(first + i * 4 + q, first + i * 4 + q + 1)
             e, v = p_ref[0, row, :], p_ref[1, row, :]
             parts.append(jnp.concatenate([jnp.where(e == cell, v, 0.0) for cell in cells], axis=1))
         sent = both_sides(jnp.concatenate(parts, axis=0), c_ref)
@@ -137,39 +137,40 @@
     return [(ref, r) for ref in parts for r in range(ref.shape[0])]
 
 
-def summed_row(held, row, cell, distinct):
-    total = jnp.zeros((BLK, 128), jnp.float32)
+def chosen_row(held, row):
+    cells = [cell.astype(jnp.bfloat16) for cell in cells_of()]
+    high = [jnp.zeros((BLK, 128), jnp.bfloat16)] * 2
+    low = list(high)
     for ref, r in held:
-        here = ref[r, 0, row, :] == cell
-        value = ref[r, 1, row, :]
-        total = jnp.where(here, value, total) if distinct else total + jnp.where(here, value, 0.0)
-    return total
-
-
-def add_kernel(*refs, distinct, before):
+        place = jnp.broadcast_to(ref[r, 0, row, :], (16, 128)).astype(jnp.bfloat16)
+        value = jnp.broadcast_to(ref[r, 1, row, :], (16, 128))
+        top = value.astype(jnp.bfloat16)
+        rest = (value - top.astype(jnp.float32)).astype(jnp.bfloat16)
+        place, top, rest = (jnp.concatenate([x] * (BLK // 16), axis=0) for x in (place, top, rest))
+        for half in range(2):
+            here = place == cells[half]
+            high[half] = jnp.where(here, top, high[half])
+            low[half] = jnp.where(here, rest, low[half])
+    return jnp.concatenate(high, axis=1).astype(jnp.float32) + jnp.concatenate(low, axis=1).astype(jnp.float32)
+
+
+def add_kernel(*refs):
     *parts, s_ref = refs
-    before_ref = parts.pop() if before else None
     held = replicas_of(parts)
     first = pl.program_id(0) * (WIDE // BLK)
-    cells = cells_of()
 
     @pl.loop(0, WIDE // BLK)
     def _(q):
-        rows = pl.ds(pl.multiple_of(q * BLK, BLK), BLK)
-        for half in range(2):
-            lanes = slice(half * 128, half * 128 + 128)
-            total = summed_row(held, pl.ds(first + q, 1), cells[half], distinct)
-            s_ref[rows, lanes] = total + before_ref[rows, lanes] if before else total
+        s_ref[pl.ds(pl.multiple_of(q * BLK, BLK), BLK), :] = chosen_row(held, pl.ds(first + q, 1))
 
 
 def late_tiles(p_ref, before_ref, c_ref, o_ref, first, scale):
     held = replicas_of([p_ref])
-    cells = cells_of()
     for i in range(WIDE // TILE):
         parts = []
         for q in range(4):
             row = slice(first + i * 4 + q, first + i * 4 + q + 1)
-            parts.append(jnp.concatenate([summed_row(held, row, cell, True) for cell in cells], axis=1))
+            parts.append(chosen_row(held, row))
         summed = before_ref[tile(i), :] + jnp.concatenate(parts, axis=0)
         out = both_sides(summed, c_ref)
         o_ref[:, tile(i)] = out if scale is None else out * scale
@@ -206,6 +207,7 @@
 
 
 VMEM_LIMIT = 32 * 1024 * 1024
+SMALLER = 55 * 1024 * 1024
 MIDDLE = 59 * 1024 * 1024
 BIG = 60 * 1024 * 1024
 
@@ -244,19 +246,26 @@
         compiler_params=params(BIG),
         cost_estimate=cost(8),
     )(momentum, gradient, places, forward)
-    three = jnp.stack([shift(packet, 1, 0), packet, shift(packet, -1, 0)])
+    opposite = lax.optimization_barrier(-packet)
+    three = jnp.stack([shift(packet, 1, 0), -opposite, shift(packet, -1, 0)])
     far = [shift(three, 3, 0), shift(three, -3, 0)]
     three_x = across(three)
     packet, three = lax.optimization_barrier((packet, three))
-    residual = pl.pallas_call(
-        residual_kernel,
-        grid=(steps,),
-        in_specs=[field_spec, field_spec, packet_spec, const_spec],
-        out_specs=field_spec,
-        out_shape=jax.ShapeDtypeStruct(momentum.shape, jnp.float32),
-        compiler_params=params(MIDDLE),
-        cost_estimate=cost(8),
-    )(momentum, gradient, packet, inverse)
+
+    def residual_part(part, into):
+        half = pl.BlockSpec((1, ROWS, WIDE), lambda j: (0, 0, part))
+        return pl.pallas_call(
+            functools.partial(residual_kernel, first=part * (WIDE // BLK)),
+            grid=(1,),
+            in_specs=[half, half, packet_spec, const_spec] + [pl.BlockSpec(memory_space=pl.ANY)] * len(into),
+            out_specs=half,
+            out_shape=jax.ShapeDtypeStruct(momentum.shape, jnp.float32),
+            input_output_aliases={4: 0} if into else {},
+            compiler_params=params(SMALLER if into else MIDDLE),
+            cost_estimate=cost(4),
+        )(momentum, gradient, packet, inverse, *into)
+
+    residual = residual_part(0, [])
     residual, *far = lax.optimization_barrier((residual, *far))
     five = jnp.concatenate([far[0], far[1][:2]])
     five_x = across(five)
@@ -278,21 +287,19 @@
             cost_estimate=cost(us),
         )(*parts)
 
-    def add_call(parts, before, distinct, us):
-        return pl.pallas_call(
-            functools.partial(add_kernel, distinct=distinct, before=len(before) > 0),
-            grid=(steps,),
-            in_specs=[whole(x.shape) for x in parts] + [sum_spec] * len(before),
-            out_specs=sum_spec,
-            out_shape=jax.ShapeDtypeStruct((width, TILE), jnp.float32),
-            input_output_aliases={len(parts): 0} if before else {},
-            compiler_params=params(),
-            cost_estimate=cost(us),
-        )(*parts, *before)
-
     (early_merged,) = merge_call([early], 1, distinct=False, merged=1, squared=False)
-    summed = add_call([early_merged], [], True, 5)
-    summed, *five_x = lax.optimization_barrier((summed, *five_x))
+    summed = pl.pallas_call(
+        add_kernel,
+        grid=(steps,),
+        in_specs=[whole(early_merged.shape)],
+        out_specs=sum_spec,
+        out_shape=jax.ShapeDtypeStruct((width, TILE), jnp.float32),
+        compiler_params=params(),
+        cost_estimate=cost(5),
+    )(early_merged)
+    residual, five = lax.optimization_barrier((residual, five))
+    residual = residual_part(1, [residual])
+    summed, residual, *five_x = lax.optimization_barrier((summed, residual, *five_x))
     merged, squares = merge_call([five_x, [early_merged]], 2, distinct=True, merged=1, squared=True)
     total = tensor_sum(squares)
     half_shape = jax.ShapeDtypeStruct((ROWS, WIDE), jnp.float32)

time: 68 us -> 66.8 us (0.982)
  waiting for transfers between devices: 14.3 us -> 10.5 us
  Pallas kernels: 29.4 us -> 31.9 us
    ppermute x10, waiting for transfers between devices: 12.8 us -> 8.56 us  [shift(): return lax.ppermute(x, 'dp', pairs)]
    pallas_call x2 -> x3, Pallas kernels: 11.6 us -> 15 us  [the longest x2 10.3 us: residual_part(): pl.pallas_call(functools.partial(residual_kernel, first=part * (WIDE // B...]
    neg x0 -> x1, other arithmetic: none -> 0.86 us  [shards(): opposite = lax.optimization_barrier(-packet)]
    another operation x1 -> x2, other arithmetic: 0.83 us -> 0.02 us  [shards(): three = jnp.stack([shift(packet, 1, 0), -opposite, shift(packet, -1, 0)])]
  transfers between devices with their start and end apart: 14 -> 14, of which waited for: 7 -> 6; matrix products, arithmetic and copies ran while one was open for 0% -> 1% of each run, Pallas kernels for 23% -> 28%
where the time goes in v2:
time: 66.8 us; the launch traced here: 66.7 us
  Pallas kernels  31.9 us (48%)
  starting transfers between devices  22.6 us (34%)
  waiting for transfers between devices  10.5 us (16%)
  other arithmetic  0.92 us (1%)
  between operations  0.7 us (1%)
    ppermute x10, starting transfers between devices, shift(): return lax.ppermute(x, 'dp', pairs)  17.3 us
    pallas_call x2, Pallas kernels, residual_part(): pl.pallas_call(functools.partial(residual_kernel, first=part * (WIDE // B...  10.3 us
    ppermute x10, waiting for transfers between devices, shift(): return lax.ppermute(x, 'dp', pairs)  8.56 us
    pallas_call x1, Pallas kernels, shards(): pl.pallas_call(values_kernel, grid=(steps,), in_specs=[field_spec, field_...  6.62 us
    ppermute x3, starting transfers between devices, tensor_sum(): lax.ppermute(x, 'tensor', [(t, (t + k) % T) for t in range(T)])  5.22 us
    pallas_call x1, Pallas kernels, shards(): pl.pallas_call(right_kernel, grid=(2,), in_specs=[whole(merged.shape), pl...  5.07 us
    pallas_call x1, Pallas kernels, shards(): pl.pallas_call(add_kernel, grid=(steps,), in_specs=[whole(early_merged.sh...  4.62 us
    pallas_call x1, Pallas kernels, shards(): pl.pallas_call(left_kernel, grid=(1,), in_specs=[whole(merged.shape), pl....  3.05 us
  transfers between devices with their start and end apart: 14, of which 6 were waited for; matrix products, arithmetic and copies ran while one was open for 1% of the time, Pallas kernels for 28%

profile of v2, /device:TPU:32, one launch (start us, length us, event | category | flops | bytes accessed | tf_op | source)
XLA Modules:
  0.0 66.7 jit_solution(2359686791474780177)
XLA Ops:
  0.6 6.6 %shard_map.68.p_ref = f32[2,56,128]{2,1,0:T(8,128)} custom-call(f32[1,256,3584]{2,1,0:T(8,128)} %m_ref.5, bf16[1,256,3584]{2,1,0:T(8,128)(2,1)} %g_ref.5, s32[128,56]{1,0:T(8,128)} %bitcast.11, bf16[2,768,256]{2,1,0:T(8,128)(2,1)} %constant.4.clone.c_ref), custom_call_target="tpu_custom_call" | custom-call | flops 8000000000 | bytes 28000000 | tf_op jit(solution)/shard_map/pallas_call | solution.py:240
  7.2 1.8 %collective-permute-start.1 = (f32[2,56,128]{2,1,0:T(8,128)}, f32[2,56,128]{2,1,0:T(8,128)S(1)}, u32[]{:S(2)}, u32[]{:S(2)}) collective-permute-start(f32[2,56,128]{2,1,0:T(8,128)} %shard_map.68.p_ref), channel_id=1, source_target_pairs={{0,224},{8,232},{16,240},{24,248},{32,0},{40,8},{48,16},{56,24},{6... | collective-permute-start | bytes 172040 | tf_op jit(solution)/shard_map/ppermute | solution.py:206
  9.1 0.2 collective-permute-start
  9.3 0.9 %neg.6 = f32[2,56,128]{2,1,0:T(8,128)S(1)} negate(f32[2,56,128]{2,1,0:T(8,128)} %shard_map.68.p_ref) | non-fusion elementwise | flops 14336 | bytes 114688 | tf_op jit(solution)/shard_map/neg | solution.py:249
  10.1 1.5 %collective-permute-done.1 = f32[2,56,128]{2,1,0:T(8,128)S(1)} collective-permute-done((f32[2,56,128]{2,1,0:T(8,128)}, f32[2,56,128]{2,1,0:T(8,128)S(1)}, u32[]{:S(2)}, u32[]{:S(2)}) %collective-permute-start.1) | collective-permute-done | bytes 57376 | tf_op jit(solution)/shard_map/ppermute | solution.py:206
  11.6 4.0 %collective-permute-done = f32[2,56,128]{2,1,0:T(8,128)S(1)} collective-permute-done((f32[2,56,128]{2,1,0:T(8,128)}, f32[2,56,128]{2,1,0:T(8,128)S(1)}, u32[]{:S(2)}, u32[]{:S(2)}) %collective-permute-start) | collective-permute-done | bytes 57376 | tf_op jit(solution)/shard_map/ppermute | solution.py:206
  15.6 3.0 %collective-permute-start.6 = (f32[3,2,56,128]{3,2,1,0:T(8,128)S(1)}, f32[3,2,56,128]{3,2,1,0:T(8,128)S(1)}, u32[]{:S(2)}, u32[]{:S(2)}) collective-permute-start(f32[3,2,56,128]{3,2,1,0:T(8,128)S(1)} %pad_maximum_fusion.1.refs_0_), channel_id=1, source_target_pairs={{0,160},{8,168},{16,176},{24,184},{32,192},{40,200},{48,208},{56,2... | collective-permute-start | bytes 516104 | tf_op jit(solution)/shard_map/ppermute | solution.py:206
  18.6 2.2 %collective-permute-start.5 = (f32[3,2,56,128]{3,2,1,0:T(8,128)S(1)}, f32[3,2,56,128]{3,2,1,0:T(8,128)S(1)}, u32[]{:S(2)}, u32[]{:S(2)}) collective-permute-start(f32[3,2,56,128]{3,2,1,0:T(8,128)S(1)} %pad_maximum_fusion.1.refs_0_), channel_id=1, source_target_pairs={{0,96},{8,104},{16,112},{24,120},{32,128},{40,136},{48,144},{56,15... | collective-permute-start | bytes 516104 | tf_op jit(solution)/shard_map/ppermute | solution.py:206
  20.7 3.0 %collective-permute-start.4 = (f32[3,2,56,128]{3,2,1,0:T(8,128)S(1)}, f32[3,2,56,128]{3,2,1,0:T(8,128)S(1)}, u32[]{:S(2)}, u32[]{:S(2)}) collective-permute-start(f32[3,2,56,128]{3,2,1,0:T(8,128)S(1)} %pad_maximum_fusion.1.refs_0_), channel_id=1, source_target_pairs={{0,16},{8,24},{16,0},{24,8},{32,48},{40,56},{48,32},{56,40},{64,80... | collective-permute-start | bytes 516104 | tf_op jit(solution)/shard_map/ppermute | solution.py:206
  23.8 1.1 %collective-permute-start.3 = (f32[3,2,56,128]{3,2,1,0:T(8,128)S(1)}, f32[3,2,56,128]{3,2,1,0:T(8,128)S(1)}, u32[]{:S(2)}, u32[]{:S(2)}) collective-permute-start(f32[3,2,56,128]{3,2,1,0:T(8,128)S(1)} %pad_maximum_fusion.1.refs_0_), channel_id=1, source_target_pairs={{0,24},{8,0},{16,8},{24,16},{32,56},{40,32},{48,40},{56,48},{64,88... | collective-permute-start | bytes 516104 | tf_op jit(solution)/shard_map/ppermute | solution.py:206
  24.9 0.9 %collective-permute-start.2 = (f32[3,2,56,128]{3,2,1,0:T(8,128)S(1)}, f32[3,2,56,128]{3,2,1,0:T(8,128)S(1)}, u32[]{:S(2)}, u32[]{:S(2)}) collective-permute-start(f32[3,2,56,128]{3,2,1,0:T(8,128)S(1)} %pad_maximum_fusion.1.refs_0_), channel_id=1, source_target_pairs={{0,8},{8,16},{16,24},{24,0},{32,40},{40,48},{48,56},{56,32},{64,72... | collective-permute-start | bytes 516104 | tf_op jit(solution)/shard_map/ppermute | solution.py:206
  25.8 5.2 %shard_map.69.rest_0_ = f32[1,256,3584]{2,1,0:T(8,128)} custom-call(f32[1,256,3584]{2,1,0:T(8,128)} %m_ref.5, bf16[1,256,3584]{2,1,0:T(8,128)(2,1)} %g_ref.5, f32[2,56,128]{2,1,0:T(8,128)} %shard_map.68.p_ref, bf16[2,768,256]{2,1,0:T(8,128)(2,1)} %constant.5.clone.c_ref), custom_call_target="tpu_custom_call" | custom-call | flops 4000000000 | bytes 14000000 | tf_op jit(solution)/shard_map/pallas_call | solution.py:257
  31.0 0.0 collective-permute-done.6
  31.0 2.1 %collective-permute-done.5 = f32[3,2,56,128]{3,2,1,0:T(8,128)S(1)} collective-permute-done((f32[3,2,56,128]{3,2,1,0:T(8,128)S(1)}, f32[3,2,56,128]{3,2,1,0:T(8,128)S(1)}, u32[]{:S(2)}, u32[]{:S(2)}) %collective-permute-start.5) | collective-permute-done | bytes 172064 | tf_op jit(solution)/shard_map/ppermute | solution.py:206
  33.1 3.1 %collective-permute-start.9 = (f32[5,2,56,128]{3,2,1,0:T(8,128)S(1)}, f32[5,2,56,128]{3,2,1,0:T(8,128)S(1)}, u32[]{:S(2)}, u32[]{:S(2)}) collective-permute-start(f32[5,2,56,128]{3,2,1,0:T(8,128)S(1)} %pad_maximum_fusion.refs_4_), channel_id=1, source_target_pairs={{0,16},{8,24},{16,0},{24,8},{32,48},{40,56},{48,32},{56,40},{64,80... | collective-permute-start | bytes 860168 | tf_op jit(solution)/shard_map/ppermute | solution.py:206
  36.2 1.1 %collective-permute-start.8 = (f32[5,2,56,128]{3,2,1,0:T(8,128)S(1)}, f32[5,2,56,128]{3,2,1,0:T(8,128)S(1)}, u32[]{:S(2)}, u32[]{:S(2)}) collective-permute-start(f32[5,2,56,128]{3,2,1,0:T(8,128)S(1)} %pad_maximum_fusion.refs_4_), channel_id=1, source_target_pairs={{0,24},{8,0},{16,8},{24,16},{32,56},{40,32},{48,40},{56,48},{64,88... | collective-permute-start | bytes 860168 | tf_op jit(solution)/shard_map/ppermute | solution.py:206
  37.3 0.9 %collective-permute-start.7 = (f32[5,2,56,128]{3,2,1,0:T(8,128)S(1)}, f32[5,2,56,128]{3,2,1,0:T(8,128)S(1)}, u32[]{:S(2)}, u32[]{:S(2)}) collective-permute-start(f32[5,2,56,128]{3,2,1,0:T(8,128)S(1)} %pad_maximum_fusion.refs_4_), channel_id=1, source_target_pairs={{0,8},{8,16},{16,24},{24,0},{32,40},{40,48},{48,56},{56,32},{64,72... | collective-permute-start | bytes 860168 | tf_op jit(solution)/shard_map/ppermute | solution.py:206
  38.2 0.0 collective-permute-done.3.refs_2_
  38.2 0.0 collective-permute-done.2.refs_1_
  38.2 0.5 shard_map.70.refs_0_.refs_3_
  38.8 4.6 %shard_map.71.before_ref = f32[3584,256]{1,0:T(8,128)S(1)} custom-call(f32[17,2,56,128]{3,2,1,0:T(8,128)S(1)} %shard_map.70.refs_0_.refs_3_), custom_call_target="tpu_custom_call" | custom-call | flops 5000000000 | bytes 17500000 | tf_op jit(solution)/shard_map/pallas_call | solution.py:291
  43.4 5.2 %shard_map.72 = f32[1,256,3584]{2,1,0:T(8,128)} custom-call(f32[1,256,3584]{2,1,0:T(8,128)} %m_ref.5, bf16[1,256,3584]{2,1,0:T(8,128)(2,1)} %g_ref.5, f32[2,56,128]{2,1,0:T(8,128)} %shard_map.68.p_ref, bf16[2,768,256]{2,1,0:T(8,128)(2,1)} %constant.5.clone.c_ref, f32[1,256,3584]{2,1,0:T(8,128)} %shard_map.69.rest_0_), custom_call_target="tpu_custom_call", output_to_operand_aliasing={{}: (4, {})} | custom-call | flops 4000000000 | bytes 14000000 | tf_op jit(solution)/shard_map/pallas_call | solution.py:257
  48.6 1.0 %collective-permute-done.8.refs_1_ = f32[5,2,56,128]{3,2,1,0:T(8,128)S(1)} collective-permute-done((f32[5,2,56,128]{3,2,1,0:T(8,128)S(1)}, f32[5,2,56,128]{3,2,1,0:T(8,128)S(1)}, u32[]{:S(2)}, u32[]{:S(2)}) %collective-permute-start.8) | collective-permute-done | bytes 286752 | tf_op jit(solution)/shard_map/ppermute | solution.py:206
  49.6 1.7 %shard_map.73 = (f32[15,2,56,128]{3,2,1,0:T(8,128)S(1)}, f32[8,128]{1,0:T(8,128)S(1)}) custom-call(f32[5,2,56,128]{3,2,1,0:T(8,128)S(1)} %collective-permute-done.7.refs_0_, f32[5,2,56,128]{3,2,1,0:T(8,128)S(1)} %collective-permute-done.8.refs_1_, f32[5,2,56,128]{3,2,1,0:T(8,128)S(1)} %collective-permute-done.9.refs_2_, ...), custom_call_target="tpu_custom_call" | custom-call | flops 2000000000 | bytes 7000000 | tf_op jit(solution)/shard_map/pallas_call | solution.py:283
  51.3 0.1 collective-permute-start.10
  51.4 1.2 %collective-permute-done.10 = f32[8,128]{1,0:T(8,128)S(1)} collective-permute-done((f32[8,128]{1,0:T(8,128)S(1)}, f32[8,128]{1,0:T(8,128)S(1)}, u32[]{:S(2)}, u32[]{:S(2)}) %collective-permute-start.10) | collective-permute-done | bytes 4128 | tf_op jit(solution)/shard_map/ppermute | solution.py:200
  52.5 3.2 %collective-permute-start.13 = (f32[8,128]{1,0:T(8,128)S(1)}, f32[8,128]{1,0:T(8,128)S(1)}, u32[]{:S(2)}, u32[]{:S(2)}) collective-permute-start(f32[8,128]{1,0:T(8,128)S(1)} %add.12), channel_id=1, source_target_pairs={{0,4},{1,5},{2,6},{3,7},{4,0},{5,1},{6,2},{7,3},{8,12},{9,13},{10,... | collective-permute-start | bytes 12296 | tf_op jit(solution)/shard_map/ppermute | solution.py:201
  55.7 1.1 %collective-permute-start.12 = (f32[8,128]{1,0:T(8,128)S(1)}, f32[8,128]{1,0:T(8,128)S(1)}, u32[]{:S(2)}, u32[]{:S(2)}) collective-permute-start(f32[8,128]{1,0:T(8,128)S(1)} %add.12), channel_id=1, source_target_pairs={{0,6},{1,7},{2,0},{3,1},{4,2},{5,3},{6,4},{7,5},{8,14},{9,15},{10,... | collective-permute-start | bytes 12296 | tf_op jit(solution)/shard_map/ppermute | solution.py:201
  56.8 1.0 %collective-permute-start.11 = (f32[8,128]{1,0:T(8,128)S(1)}, f32[8,128]{1,0:T(8,128)S(1)}, u32[]{:S(2)}, u32[]{:S(2)}) collective-permute-start(f32[8,128]{1,0:T(8,128)S(1)} %add.12), channel_id=1, source_target_pairs={{0,2},{1,3},{2,4},{3,5},{4,6},{5,7},{6,0},{7,1},{8,10},{9,11},{10,... | collective-permute-start | bytes 12296 | tf_op jit(solution)/shard_map/ppermute | solution.py:201
  57.7 3.0 %shard_map.74.x_ref = f32[256,1792]{1,0:T(8,128)S(1)} custom-call(f32[15,2,56,128]{3,2,1,0:T(8,128)S(1)} %get-tuple-element.26.p_ref, f32[3584,256]{1,0:T(8,128)S(1)} %shard_map.71.before_ref, bf16[2,768,256]{2,1,0:T(8,128)(2,1)S(1)} %copy-done), custom_call_target="tpu_custom_call" | custom-call | flops 4000000000 | bytes 14000000 | tf_op jit(solution)/shard_map/pallas_call | solution.py:307
  60.8 0.8 %collective-permute-done.11 = f32[8,128]{1,0:T(8,128)S(1)} collective-permute-done((f32[8,128]{1,0:T(8,128)S(1)}, f32[8,128]{1,0:T(8,128)S(1)}, u32[]{:S(2)}, u32[]{:S(2)}) %collective-permute-start.11) | collective-permute-done | bytes 4128 | tf_op jit(solution)/shard_map/ppermute | solution.py:201
  61.6 5.1 %shard_map.75 = f32[256,3584]{1,0:T(8,128)} custom-call(f32[15,2,56,128]{3,2,1,0:T(8,128)S(1)} %get-tuple-element.26.p_ref, f32[3584,256]{1,0:T(8,128)S(1)} %shard_map.71.before_ref, bf16[2,768,256]{2,1,0:T(8,128)(2,1)S(1)} %copy-done, f32[256,1792]{1,0:T(8,128)S(1)} %shard_map.74.x_ref, f32[8,128]{1,0:T(8,128)S(1)} %add_add_fusion.total_ref), custom_call_target="tpu_custom_call" | custom-call | flops 5000000000 | bytes 17500000 | tf_op jit(solution)/shard_map/pallas_call | solution.py:317
  (13 shorter events, 0.1 us)
Async XLA Ops:
  7.2 4.4 %collective-permute-start.1 = (f32[2,56,128]{2,1,0:T(8,128)}, f32[2,56,128]{2,1,0:T(8,128)S(1)}, u32[]{:S(2)}, u32[]{:S(2)}) collective-permute-start(f32[2,56,128]{2,1,0:T(8,128)} %shard_map.68.p_ref), channel_id=1, source_target_pairs={{0,224},{8,232},{16,240},{24,248},{32,0},{40,8},{48,16},{56,24},{6... | collective-permute-start | bytes 172040 | tf_op jit(solution)/shard_map/ppermute | solution.py:206
  9.1 6.5 %collective-permute-start = (f32[2,56,128]{2,1,0:T(8,128)}, f32[2,56,128]{2,1,0:T(8,128)S(1)}, u32[]{:S(2)}, u32[]{:S(2)}) collective-permute-start(f32[2,56,128]{2,1,0:T(8,128)} %shard_map.68.p_ref), channel_id=1, source_target_pairs={{0,32},{8,40},{16,48},{24,56},{32,64},{40,72},{48,80},{56,88},{64,... | collective-permute-start | bytes 172040 | tf_op jit(solution)/shard_map/ppermute | solution.py:206
  15.6 15.3 %collective-permute-start.6 = (f32[3,2,56,128]{3,2,1,0:T(8,128)S(1)}, f32[3,2,56,128]{3,2,1,0:T(8,128)S(1)}, u32[]{:S(2)}, u32[]{:S(2)}) collective-permute-start(f32[3,2,56,128]{3,2,1,0:T(8,128)S(1)} %pad_maximum_fusion.1.refs_0_), channel_id=1, source_target_pairs={{0,160},{8,168},{16,176},{24,184},{32,192},{40,200},{48,208},{56,2... | collective-permute-start | bytes 516104 | tf_op jit(solution)/shard_map/ppermute | solution.py:206
  18.6 14.4 %collective-permute-start.5 = (f32[3,2,56,128]{3,2,1,0:T(8,128)S(1)}, f32[3,2,56,128]{3,2,1,0:T(8,128)S(1)}, u32[]{:S(2)}, u32[]{:S(2)}) collective-permute-start(f32[3,2,56,128]{3,2,1,0:T(8,128)S(1)} %pad_maximum_fusion.1.refs_0_), channel_id=1, source_target_pairs={{0,96},{8,104},{16,112},{24,120},{32,128},{40,136},{48,144},{56,15... | collective-permute-start | bytes 516104 | tf_op jit(solution)/shard_map/ppermute | solution.py:206
  20.7 16.6 %collective-permute-start.4 = (f32[3,2,56,128]{3,2,1,0:T(8,128)S(1)}, f32[3,2,56,128]{3,2,1,0:T(8,128)S(1)}, u32[]{:S(2)}, u32[]{:S(2)}) collective-permute-start(f32[3,2,56,128]{3,2,1,0:T(8,128)S(1)} %pad_maximum_fusion.1.refs_0_), channel_id=1, source_target_pairs={{0,16},{8,24},{16,0},{24,8},{32,48},{40,56},{48,32},{56,40},{64,80... | collective-permute-start | bytes 516104 | tf_op jit(solution)/shard_map/ppermute | solution.py:206
  23.8 14.4 %collective-permute-start.3 = (f32[3,2,56,128]{3,2,1,0:T(8,128)S(1)}, f32[3,2,56,128]{3,2,1,0:T(8,128)S(1)}, u32[]{:S(2)}, u32[]{:S(2)}) collective-permute-start(f32[3,2,56,128]{3,2,1,0:T(8,128)S(1)} %pad_maximum_fusion.1.refs_0_), channel_id=1, source_target_pairs={{0,24},{8,0},{16,8},{24,16},{32,56},{40,32},{48,40},{56,48},{64,88... | collective-permute-start | bytes 516104 | tf_op jit(solution)/shard_map/ppermute | solution.py:206
  24.9 13.3 %collective-permute-start.2 = (f32[3,2,56,128]{3,2,1,0:T(8,128)S(1)}, f32[3,2,56,128]{3,2,1,0:T(8,128)S(1)}, u32[]{:S(2)}, u32[]{:S(2)}) collective-permute-start(f32[3,2,56,128]{3,2,1,0:T(8,128)S(1)} %pad_maximum_fusion.1.refs_0_), channel_id=1, source_target_pairs={{0,8},{8,16},{16,24},{24,0},{32,40},{40,48},{48,56},{56,32},{64,72... | collective-permute-start | bytes 516104 | tf_op jit(solution)/shard_map/ppermute | solution.py:206
  33.1 15.5 %collective-permute-start.9 = (f32[5,2,56,128]{3,2,1,0:T(8,128)S(1)}, f32[5,2,56,128]{3,2,1,0:T(8,128)S(1)}, u32[]{:S(2)}, u32[]{:S(2)}) collective-permute-start(f32[5,2,56,128]{3,2,1,0:T(8,128)S(1)} %pad_maximum_fusion.refs_4_), channel_id=1, source_target_pairs={{0,16},{8,24},{16,0},{24,8},{32,48},{40,56},{48,32},{56,40},{64,80... | collective-permute-start | bytes 860168 | tf_op jit(solution)/shard_map/ppermute | solution.py:206
  36.2 13.4 %collective-permute-start.8 = (f32[5,2,56,128]{3,2,1,0:T(8,128)S(1)}, f32[5,2,56,128]{3,2,1,0:T(8,128)S(1)}, u32[]{:S(2)}, u32[]{:S(2)}) collective-permute-start(f32[5,2,56,128]{3,2,1,0:T(8,128)S(1)} %pad_maximum_fusion.refs_4_), channel_id=1, source_target_pairs={{0,24},{8,0},{16,8},{24,16},{32,56},{40,32},{48,40},{56,48},{64,88... | collective-permute-start | bytes 860168 | tf_op jit(solution)/shard_map/ppermute | solution.py:206
  37.3 12.3 %collective-permute-start.7 = (f32[5,2,56,128]{3,2,1,0:T(8,128)S(1)}, f32[5,2,56,128]{3,2,1,0:T(8,128)S(1)}, u32[]{:S(2)}, u32[]{:S(2)}) collective-permute-start(f32[5,2,56,128]{3,2,1,0:T(8,128)S(1)} %pad_maximum_fusion.refs_4_), channel_id=1, source_target_pairs={{0,8},{8,16},{16,24},{24,0},{32,40},{40,48},{48,56},{56,32},{64,72... | collective-permute-start | bytes 860168 | tf_op jit(solution)/shard_map/ppermute | solution.py:206
  48.6 9.2 %copy-start = (bf16[2,768,256]{2,1,0:T(8,128)(2,1)S(1)}, bf16[2,768,256]{2,1,0:T(8,128)(2,1)}, u32[]{:S(2)}) copy-start(bf16[2,768,256]{2,1,0:T(8,128)(2,1)} %constant.5.clone.c_ref) | copy-start | bytes 2359300
  51.3 1.2 %collective-permute-start.10 = (f32[8,128]{1,0:T(8,128)S(1)}, f32[8,128]{1,0:T(8,128)S(1)}, u32[]{:S(2)}, u32[]{:S(2)}) collective-permute-start(f32[8,128]{1,0:T(8,128)S(1)} %get-tuple-element.28), channel_id=1, source_target_pairs={{0,1},{1,0},{2,3},{3,2},{4,5},{5,4},{6,7},{7,6},{8,9},{9,8},{10,11... | collective-permute-start | bytes 12296 | tf_op jit(solution)/shard_map/ppermute | solution.py:200
  52.5 8.3 %collective-permute-start.13 = (f32[8,128]{1,0:T(8,128)S(1)}, f32[8,128]{1,0:T(8,128)S(1)}, u32[]{:S(2)}, u32[]{:S(2)}) collective-permute-start(f32[8,128]{1,0:T(8,128)S(1)} %add.12), channel_id=1, source_target_pairs={{0,4},{1,5},{2,6},{3,7},{4,0},{5,1},{6,2},{7,3},{8,12},{9,13},{10,... | collective-permute-start | bytes 12296 | tf_op jit(solution)/shard_map/ppermute | solution.py:201
  55.7 5.1 %collective-permute-start.12 = (f32[8,128]{1,0:T(8,128)S(1)}, f32[8,128]{1,0:T(8,128)S(1)}, u32[]{:S(2)}, u32[]{:S(2)}) collective-permute-start(f32[8,128]{1,0:T(8,128)S(1)} %add.12), channel_id=1, source_target_pairs={{0,6},{1,7},{2,0},{3,1},{4,2},{5,3},{6,4},{7,5},{8,14},{9,15},{10,... | collective-permute-start | bytes 12296 | tf_op jit(solution)/shard_map/ppermute | solution.py:201
  56.8 4.8 %collective-permute-start.11 = (f32[8,128]{1,0:T(8,128)S(1)}, f32[8,128]{1,0:T(8,128)S(1)}, u32[]{:S(2)}, u32[]{:S(2)}) collective-permute-start(f32[8,128]{1,0:T(8,128)S(1)} %add.12), channel_id=1, source_target_pairs={{0,2},{1,3},{2,4},{3,5},{4,6},{5,7},{6,0},{7,1},{8,10},{9,11},{10,... | collective-permute-start | bytes 12296 | tf_op jit(solution)/shard_map/ppermute | solution.py:201

commit v3 on v2

--- a/solution.py
+++ b/solution.py
@@ -159,9 +159,11 @@
     held = replicas_of(parts)
     first = pl.program_id(0) * (WIDE // BLK)
 
-    @pl.loop(0, WIDE // BLK)
-    def _(q):
-        s_ref[pl.ds(pl.multiple_of(q * BLK, BLK), BLK), :] = chosen_row(held, pl.ds(first + q, 1))
+    @pl.loop(0, WIDE // TILE)
+    def _(i):
+        for u in range(4):
+            q = i * 4 + u
+            s_ref[pl.ds(pl.multiple_of(q * BLK, BLK), BLK), :] = chosen_row(held, pl.ds(first + q, 1))
 
 
 def late_tiles(p_ref, before_ref, c_ref, o_ref, first, scale):

time: 66.8 us -> 66.8 us (level)
  transfers between devices with their start and end apart: 14 -> 14, of which waited for: 6 -> 6; matrix products, arithmetic and copies ran while one was open for 1% -> 1% of each run, Pallas kernels for 28% -> 27%
where the time goes in v3:
time: 66.8 us; the launch traced here: 66.7 us
  Pallas kernels  31.5 us (47%)
  starting transfers between devices  22.6 us (34%)
  waiting for transfers between devices  10.9 us (16%)
  other arithmetic  0.92 us (1%)
  between operations  0.7 us (1%)
    ppermute x10, starting transfers between devices, shift(): return lax.ppermute(x, 'dp', pairs)  17.3 us
    pallas_call x2, Pallas kernels, residual_part(): pl.pallas_call(functools.partial(residual_kernel, first=part * (WIDE // B...  10.3 us
    ppermute x10, waiting for transfers between devices, shift(): return lax.ppermute(x, 'dp', pairs)  8.99 us
    pallas_call x1, Pallas kernels, shards(): pl.pallas_call(values_kernel, grid=(steps,), in_specs=[field_spec, field_...  6.62 us
    ppermute x3, starting transfers between devices, tensor_sum(): lax.ppermute(x, 'tensor', [(t, (t + k) % T) for t in range(T)])  5.22 us
    pallas_call x1, Pallas kernels, shards(): pl.pallas_call(right_kernel, grid=(2,), in_specs=[whole(merged.shape), pl...  5.07 us
    pallas_call x1, Pallas kernels, shards(): pl.pallas_call(add_kernel, grid=(steps,), in_specs=[whole(early_merged.sh...  4.18 us
    pallas_call x1, Pallas kernels, shards(): pl.pallas_call(left_kernel, grid=(1,), in_specs=[whole(merged.shape), pl....  3.05 us
  transfers between devices with their start and end apart: 14, of which 6 were waited for; matrix products, arithmetic and copies ran while one was open for 1% of the time, Pallas kernels for 27%

profile of v3, /device:TPU:32, one launch (start us, length us, event | category | flops | bytes accessed | tf_op | source)
XLA Modules:
  0.0 66.7 jit_solution(1268327000256124631)
XLA Ops:
  0.6 6.6 %shard_map.68.p_ref = f32[2,56,128]{2,1,0:T(8,128)} custom-call(f32[1,256,3584]{2,1,0:T(8,128)} %m_ref.5, bf16[1,256,3584]{2,1,0:T(8,128)(2,1)} %g_ref.5, s32[128,56]{1,0:T(8,128)} %bitcast.11, bf16[2,768,256]{2,1,0:T(8,128)(2,1)} %constant.4.clone.c_ref), custom_call_target="tpu_custom_call" | custom-call | flops 8000000000 | bytes 28000000 | tf_op jit(solution)/shard_map/pallas_call | solution.py:242
  7.2 1.8 %collective-permute-start.1 = (f32[2,56,128]{2,1,0:T(8,128)}, f32[2,56,128]{2,1,0:T(8,128)S(1)}, u32[]{:S(2)}, u32[]{:S(2)}) collective-permute-start(f32[2,56,128]{2,1,0:T(8,128)} %shard_map.68.p_ref), channel_id=1, source_target_pairs={{0,224},{8,232},{16,240},{24,248},{32,0},{40,8},{48,16},{56,24},{6... | collective-permute-start | bytes 172040 | tf_op jit(solution)/shard_map/ppermute | solution.py:208
  9.1 0.2 collective-permute-start
  9.3 0.9 %neg.6 = f32[2,56,128]{2,1,0:T(8,128)S(1)} negate(f32[2,56,128]{2,1,0:T(8,128)} %shard_map.68.p_ref) | non-fusion elementwise | flops 14336 | bytes 114688 | tf_op jit(solution)/shard_map/neg | solution.py:251
  10.1 1.5 %collective-permute-done.1 = f32[2,56,128]{2,1,0:T(8,128)S(1)} collective-permute-done((f32[2,56,128]{2,1,0:T(8,128)}, f32[2,56,128]{2,1,0:T(8,128)S(1)}, u32[]{:S(2)}, u32[]{:S(2)}) %collective-permute-start.1) | collective-permute-done | bytes 57376 | tf_op jit(solution)/shard_map/ppermute | solution.py:208
  11.6 4.0 %collective-permute-done = f32[2,56,128]{2,1,0:T(8,128)S(1)} collective-permute-done((f32[2,56,128]{2,1,0:T(8,128)}, f32[2,56,128]{2,1,0:T(8,128)S(1)}, u32[]{:S(2)}, u32[]{:S(2)}) %collective-permute-start) | collective-permute-done | bytes 57376 | tf_op jit(solution)/shard_map/ppermute | solution.py:208
  15.6 3.0 %collective-permute-start.6 = (f32[3,2,56,128]{3,2,1,0:T(8,128)S(1)}, f32[3,2,56,128]{3,2,1,0:T(8,128)S(1)}, u32[]{:S(2)}, u32[]{:S(2)}) collective-permute-start(f32[3,2,56,128]{3,2,1,0:T(8,128)S(1)} %pad_maximum_fusion.1.refs_0_), channel_id=1, source_target_pairs={{0,160},{8,168},{16,176},{24,184},{32,192},{40,200},{48,208},{56,2... | collective-permute-start | bytes 516104 | tf_op jit(solution)/shard_map/ppermute | solution.py:208
  18.6 2.2 %collective-permute-start.5 = (f32[3,2,56,128]{3,2,1,0:T(8,128)S(1)}, f32[3,2,56,128]{3,2,1,0:T(8,128)S(1)}, u32[]{:S(2)}, u32[]{:S(2)}) collective-permute-start(f32[3,2,56,128]{3,2,1,0:T(8,128)S(1)} %pad_maximum_fusion.1.refs_0_), channel_id=1, source_target_pairs={{0,96},{8,104},{16,112},{24,120},{32,128},{40,136},{48,144},{56,15... | collective-permute-start | bytes 516104 | tf_op jit(solution)/shard_map/ppermute | solution.py:208
  20.7 3.0 %collective-permute-start.4 = (f32[3,2,56,128]{3,2,1,0:T(8,128)S(1)}, f32[3,2,56,128]{3,2,1,0:T(8,128)S(1)}, u32[]{:S(2)}, u32[]{:S(2)}) collective-permute-start(f32[3,2,56,128]{3,2,1,0:T(8,128)S(1)} %pad_maximum_fusion.1.refs_0_), channel_id=1, source_target_pairs={{0,16},{8,24},{16,0},{24,8},{32,48},{40,56},{48,32},{56,40},{64,80... | collective-permute-start | bytes 516104 | tf_op jit(solution)/shard_map/ppermute | solution.py:208
  23.8 1.1 %collective-permute-start.3 = (f32[3,2,56,128]{3,2,1,0:T(8,128)S(1)}, f32[3,2,56,128]{3,2,1,0:T(8,128)S(1)}, u32[]{:S(2)}, u32[]{:S(2)}) collective-permute-start(f32[3,2,56,128]{3,2,1,0:T(8,128)S(1)} %pad_maximum_fusion.1.refs_0_), channel_id=1, source_target_pairs={{0,24},{8,0},{16,8},{24,16},{32,56},{40,32},{48,40},{56,48},{64,88... | collective-permute-start | bytes 516104 | tf_op jit(solution)/shard_map/ppermute | solution.py:208
  24.9 0.9 %collective-permute-start.2 = (f32[3,2,56,128]{3,2,1,0:T(8,128)S(1)}, f32[3,2,56,128]{3,2,1,0:T(8,128)S(1)}, u32[]{:S(2)}, u32[]{:S(2)}) collective-permute-start(f32[3,2,56,128]{3,2,1,0:T(8,128)S(1)} %pad_maximum_fusion.1.refs_0_), channel_id=1, source_target_pairs={{0,8},{8,16},{16,24},{24,0},{32,40},{40,48},{48,56},{56,32},{64,72... | collective-permute-start | bytes 516104 | tf_op jit(solution)/shard_map/ppermute | solution.py:208
  25.8 5.2 %shard_map.69.rest_0_ = f32[1,256,3584]{2,1,0:T(8,128)} custom-call(f32[1,256,3584]{2,1,0:T(8,128)} %m_ref.5, bf16[1,256,3584]{2,1,0:T(8,128)(2,1)} %g_ref.5, f32[2,56,128]{2,1,0:T(8,128)} %shard_map.68.p_ref, bf16[2,768,256]{2,1,0:T(8,128)(2,1)} %constant.5.clone.c_ref), custom_call_target="tpu_custom_call" | custom-call | flops 4000000000 | bytes 14000000 | tf_op jit(solution)/shard_map/pallas_call | solution.py:259
  31.0 0.0 collective-permute-done.6
  31.0 2.1 %collective-permute-done.5 = f32[3,2,56,128]{3,2,1,0:T(8,128)S(1)} collective-permute-done((f32[3,2,56,128]{3,2,1,0:T(8,128)S(1)}, f32[3,2,56,128]{3,2,1,0:T(8,128)S(1)}, u32[]{:S(2)}, u32[]{:S(2)}) %collective-permute-start.5) | collective-permute-done | bytes 172064 | tf_op jit(solution)/shard_map/ppermute | solution.py:208
  33.1 3.1 %collective-permute-start.9 = (f32[5,2,56,128]{3,2,1,0:T(8,128)S(1)}, f32[5,2,56,128]{3,2,1,0:T(8,128)S(1)}, u32[]{:S(2)}, u32[]{:S(2)}) collective-permute-start(f32[5,2,56,128]{3,2,1,0:T(8,128)S(1)} %pad_maximum_fusion.refs_4_), channel_id=1, source_target_pairs={{0,16},{8,24},{16,0},{24,8},{32,48},{40,56},{48,32},{56,40},{64,80... | collective-permute-start | bytes 860168 | tf_op jit(solution)/shard_map/ppermute | solution.py:208
  36.2 1.1 %collective-permute-start.8 = (f32[5,2,56,128]{3,2,1,0:T(8,128)S(1)}, f32[5,2,56,128]{3,2,1,0:T(8,128)S(1)}, u32[]{:S(2)}, u32[]{:S(2)}) collective-permute-start(f32[5,2,56,128]{3,2,1,0:T(8,128)S(1)} %pad_maximum_fusion.refs_4_), channel_id=1, source_target_pairs={{0,24},{8,0},{16,8},{24,16},{32,56},{40,32},{48,40},{56,48},{64,88... | collective-permute-start | bytes 860168 | tf_op jit(solution)/shard_map/ppermute | solution.py:208
  37.3 0.9 %collective-permute-start.7 = (f32[5,2,56,128]{3,2,1,0:T(8,128)S(1)}, f32[5,2,56,128]{3,2,1,0:T(8,128)S(1)}, u32[]{:S(2)}, u32[]{:S(2)}) collective-permute-start(f32[5,2,56,128]{3,2,1,0:T(8,128)S(1)} %pad_maximum_fusion.refs_4_), channel_id=1, source_target_pairs={{0,8},{8,16},{16,24},{24,0},{32,40},{40,48},{48,56},{56,32},{64,72... | collective-permute-start | bytes 860168 | tf_op jit(solution)/shard_map/ppermute | solution.py:208
  38.2 0.0 collective-permute-done.3.refs_2_
  38.2 0.0 collective-permute-done.2.refs_1_
  38.2 0.5 shard_map.70.refs_0_.refs_3_
  38.8 4.2 %shard_map.71.before_ref = f32[3584,256]{1,0:T(8,128)S(1)} custom-call(f32[17,2,56,128]{3,2,1,0:T(8,128)S(1)} %shard_map.70.refs_0_.refs_3_), custom_call_target="tpu_custom_call" | custom-call | flops 5000000000 | bytes 17500000 | tf_op jit(solution)/shard_map/pallas_call | solution.py:293
  42.9 5.2 %shard_map.72 = f32[1,256,3584]{2,1,0:T(8,128)} custom-call(f32[1,256,3584]{2,1,0:T(8,128)} %m_ref.5, bf16[1,256,3584]{2,1,0:T(8,128)(2,1)} %g_ref.5, f32[2,56,128]{2,1,0:T(8,128)} %shard_map.68.p_ref, bf16[2,768,256]{2,1,0:T(8,128)(2,1)} %constant.5.clone.c_ref, f32[1,256,3584]{2,1,0:T(8,128)} %shard_map.69.rest_0_), custom_call_target="tpu_custom_call", output_to_operand_aliasing={{}: (4, {})} | custom-call | flops 4000000000 | bytes 14000000 | tf_op jit(solution)/shard_map/pallas_call | solution.py:259
  48.1 1.5 %collective-permute-done.8.refs_1_ = f32[5,2,56,128]{3,2,1,0:T(8,128)S(1)} collective-permute-done((f32[5,2,56,128]{3,2,1,0:T(8,128)S(1)}, f32[5,2,56,128]{3,2,1,0:T(8,128)S(1)}, u32[]{:S(2)}, u32[]{:S(2)}) %collective-permute-start.8) | collective-permute-done | bytes 286752 | tf_op jit(solution)/shard_map/ppermute | solution.py:208
  49.6 1.7 %shard_map.73 = (f32[15,2,56,128]{3,2,1,0:T(8,128)S(1)}, f32[8,128]{1,0:T(8,128)S(1)}) custom-call(f32[5,2,56,128]{3,2,1,0:T(8,128)S(1)} %collective-permute-done.7.refs_0_, f32[5,2,56,128]{3,2,1,0:T(8,128)S(1)} %collective-permute-done.8.refs_1_, f32[5,2,56,128]{3,2,1,0:T(8,128)S(1)} %collective-permute-done.9.refs_2_, ...), custom_call_target="tpu_custom_call" | custom-call | flops 2000000000 | bytes 7000000 | tf_op jit(solution)/shard_map/pallas_call | solution.py:285
  51.3 0.1 collective-permute-start.10
  51.4 1.2 %collective-permute-done.10 = f32[8,128]{1,0:T(8,128)S(1)} collective-permute-done((f32[8,128]{1,0:T(8,128)S(1)}, f32[8,128]{1,0:T(8,128)S(1)}, u32[]{:S(2)}, u32[]{:S(2)}) %collective-permute-start.10) | collective-permute-done | bytes 4128 | tf_op jit(solution)/shard_map/ppermute | solution.py:202
  52.5 3.2 %collective-permute-start.13 = (f32[8,128]{1,0:T(8,128)S(1)}, f32[8,128]{1,0:T(8,128)S(1)}, u32[]{:S(2)}, u32[]{:S(2)}) collective-permute-start(f32[8,128]{1,0:T(8,128)S(1)} %add.12), channel_id=1, source_target_pairs={{0,4},{1,5},{2,6},{3,7},{4,0},{5,1},{6,2},{7,3},{8,12},{9,13},{10,... | collective-permute-start | bytes 12296 | tf_op jit(solution)/shard_map/ppermute | solution.py:203
  55.7 1.1 %collective-permute-start.12 = (f32[8,128]{1,0:T(8,128)S(1)}, f32[8,128]{1,0:T(8,128)S(1)}, u32[]{:S(2)}, u32[]{:S(2)}) collective-permute-start(f32[8,128]{1,0:T(8,128)S(1)} %add.12), channel_id=1, source_target_pairs={{0,6},{1,7},{2,0},{3,1},{4,2},{5,3},{6,4},{7,5},{8,14},{9,15},{10,... | collective-permute-start | bytes 12296 | tf_op jit(solution)/shard_map/ppermute | solution.py:203
  56.8 1.0 %collective-permute-start.11 = (f32[8,128]{1,0:T(8,128)S(1)}, f32[8,128]{1,0:T(8,128)S(1)}, u32[]{:S(2)}, u32[]{:S(2)}) collective-permute-start(f32[8,128]{1,0:T(8,128)S(1)} %add.12), channel_id=1, source_target_pairs={{0,2},{1,3},{2,4},{3,5},{4,6},{5,7},{6,0},{7,1},{8,10},{9,11},{10,... | collective-permute-start | bytes 12296 | tf_op jit(solution)/shard_map/ppermute | solution.py:203
  57.7 3.0 %shard_map.74.x_ref = f32[256,1792]{1,0:T(8,128)S(1)} custom-call(f32[15,2,56,128]{3,2,1,0:T(8,128)S(1)} %get-tuple-element.26.p_ref, f32[3584,256]{1,0:T(8,128)S(1)} %shard_map.71.before_ref, bf16[2,768,256]{2,1,0:T(8,128)(2,1)S(1)} %copy-done), custom_call_target="tpu_custom_call" | custom-call | flops 4000000000 | bytes 14000000 | tf_op jit(solution)/shard_map/pallas_call | solution.py:309
  60.8 0.8 %collective-permute-done.11 = f32[8,128]{1,0:T(8,128)S(1)} collective-permute-done((f32[8,128]{1,0:T(8,128)S(1)}, f32[8,128]{1,0:T(8,128)S(1)}, u32[]{:S(2)}, u32[]{:S(2)}) %collective-permute-start.11) | collective-permute-done | bytes 4128 | tf_op jit(solution)/shard_map/ppermute | solution.py:203
  61.6 5.1 %shard_map.75 = f32[256,3584]{1,0:T(8,128)} custom-call(f32[15,2,56,128]{3,2,1,0:T(8,128)S(1)} %get-tuple-element.26.p_ref, f32[3584,256]{1,0:T(8,128)S(1)} %shard_map.71.before_ref, bf16[2,768,256]{2,1,0:T(8,128)(2,1)S(1)} %copy-done, f32[256,1792]{1,0:T(8,128)S(1)} %shard_map.74.x_ref, f32[8,128]{1,0:T(8,128)S(1)} %add_add_fusion.total_ref), custom_call_target="tpu_custom_call" | custom-call | flops 5000000000 | bytes 17500000 | tf_op jit(solution)/shard_map/pallas_call | solution.py:319
  (13 shorter events, 0.1 us)
Async XLA Ops:
  7.2 4.4 %collective-permute-start.1 = (f32[2,56,128]{2,1,0:T(8,128)}, f32[2,56,128]{2,1,0:T(8,128)S(1)}, u32[]{:S(2)}, u32[]{:S(2)}) collective-permute-start(f32[2,56,128]{2,1,0:T(8,128)} %shard_map.68.p_ref), channel_id=1, source_target_pairs={{0,224},{8,232},{16,240},{24,248},{32,0},{40,8},{48,16},{56,24},{6... | collective-permute-start | bytes 172040 | tf_op jit(solution)/shard_map/ppermute | solution.py:208
  9.1 6.5 %collective-permute-start = (f32[2,56,128]{2,1,0:T(8,128)}, f32[2,56,128]{2,1,0:T(8,128)S(1)}, u32[]{:S(2)}, u32[]{:S(2)}) collective-permute-start(f32[2,56,128]{2,1,0:T(8,128)} %shard_map.68.p_ref), channel_id=1, source_target_pairs={{0,32},{8,40},{16,48},{24,56},{32,64},{40,72},{48,80},{56,88},{64,... | collective-permute-start | bytes 172040 | tf_op jit(solution)/shard_map/ppermute | solution.py:208
  15.6 15.3 %collective-permute-start.6 = (f32[3,2,56,128]{3,2,1,0:T(8,128)S(1)}, f32[3,2,56,128]{3,2,1,0:T(8,128)S(1)}, u32[]{:S(2)}, u32[]{:S(2)}) collective-permute-start(f32[3,2,56,128]{3,2,1,0:T(8,128)S(1)} %pad_maximum_fusion.1.refs_0_), channel_id=1, source_target_pairs={{0,160},{8,168},{16,176},{24,184},{32,192},{40,200},{48,208},{56,2... | collective-permute-start | bytes 516104 | tf_op jit(solution)/shard_map/ppermute | solution.py:208
  18.6 14.4 %collective-permute-start.5 = (f32[3,2,56,128]{3,2,1,0:T(8,128)S(1)}, f32[3,2,56,128]{3,2,1,0:T(8,128)S(1)}, u32[]{:S(2)}, u32[]{:S(2)}) collective-permute-start(f32[3,2,56,128]{3,2,1,0:T(8,128)S(1)} %pad_maximum_fusion.1.refs_0_), channel_id=1, source_target_pairs={{0,96},{8,104},{16,112},{24,120},{32,128},{40,136},{48,144},{56,15... | collective-permute-start | bytes 516104 | tf_op jit(solution)/shard_map/ppermute | solution.py:208
  20.7 16.6 %collective-permute-start.4 = (f32[3,2,56,128]{3,2,1,0:T(8,128)S(1)}, f32[3,2,56,128]{3,2,1,0:T(8,128)S(1)}, u32[]{:S(2)}, u32[]{:S(2)}) collective-permute-start(f32[3,2,56,128]{3,2,1,0:T(8,128)S(1)} %pad_maximum_fusion.1.refs_0_), channel_id=1, source_target_pairs={{0,16},{8,24},{16,0},{24,8},{32,48},{40,56},{48,32},{56,40},{64,80... | collective-permute-start | bytes 516104 | tf_op jit(solution)/shard_map/ppermute | solution.py:208
  23.8 14.4 %collective-permute-start.3 = (f32[3,2,56,128]{3,2,1,0:T(8,128)S(1)}, f32[3,2,56,128]{3,2,1,0:T(8,128)S(1)}, u32[]{:S(2)}, u32[]{:S(2)}) collective-permute-start(f32[3,2,56,128]{3,2,1,0:T(8,128)S(1)} %pad_maximum_fusion.1.refs_0_), channel_id=1, source_target_pairs={{0,24},{8,0},{16,8},{24,16},{32,56},{40,32},{48,40},{56,48},{64,88... | collective-permute-start | bytes 516104 | tf_op jit(solution)/shard_map/ppermute | solution.py:208
  24.9 13.3 %collective-permute-start.2 = (f32[3,2,56,128]{3,2,1,0:T(8,128)S(1)}, f32[3,2,56,128]{3,2,1,0:T(8,128)S(1)}, u32[]{:S(2)}, u32[]{:S(2)}) collective-permute-start(f32[3,2,56,128]{3,2,1,0:T(8,128)S(1)} %pad_maximum_fusion.1.refs_0_), channel_id=1, source_target_pairs={{0,8},{8,16},{16,24},{24,0},{32,40},{40,48},{48,56},{56,32},{64,72... | collective-permute-start | bytes 516104 | tf_op jit(solution)/shard_map/ppermute | solution.py:208
  33.1 15.1 %collective-permute-start.9 = (f32[5,2,56,128]{3,2,1,0:T(8,128)S(1)}, f32[5,2,56,128]{3,2,1,0:T(8,128)S(1)}, u32[]{:S(2)}, u32[]{:S(2)}) collective-permute-start(f32[5,2,56,128]{3,2,1,0:T(8,128)S(1)} %pad_maximum_fusion.refs_4_), channel_id=1, source_target_pairs={{0,16},{8,24},{16,0},{24,8},{32,48},{40,56},{48,32},{56,40},{64,80... | collective-permute-start | bytes 860168 | tf_op jit(solution)/shard_map/ppermute | solution.py:208
  36.2 13.4 %collective-permute-start.8 = (f32[5,2,56,128]{3,2,1,0:T(8,128)S(1)}, f32[5,2,56,128]{3,2,1,0:T(8,128)S(1)}, u32[]{:S(2)}, u32[]{:S(2)}) collective-permute-start(f32[5,2,56,128]{3,2,1,0:T(8,128)S(1)} %pad_maximum_fusion.refs_4_), channel_id=1, source_target_pairs={{0,24},{8,0},{16,8},{24,16},{32,56},{40,32},{48,40},{56,48},{64,88... | collective-permute-start | bytes 860168 | tf_op jit(solution)/shard_map/ppermute | solution.py:208
  37.3 12.3 %collective-permute-start.7 = (f32[5,2,56,128]{3,2,1,0:T(8,128)S(1)}, f32[5,2,56,128]{3,2,1,0:T(8,128)S(1)}, u32[]{:S(2)}, u32[]{:S(2)}) collective-permute-start(f32[5,2,56,128]{3,2,1,0:T(8,128)S(1)} %pad_maximum_fusion.refs_4_), channel_id=1, source_target_pairs={{0,8},{8,16},{16,24},{24,0},{32,40},{40,48},{48,56},{56,32},{64,72... | collective-permute-start | bytes 860168 | tf_op jit(solution)/shard_map/ppermute | solution.py:208
  48.1 9.6 %copy-start = (bf16[2,768,256]{2,1,0:T(8,128)(2,1)S(1)}, bf16[2,768,256]{2,1,0:T(8,128)(2,1)}, u32[]{:S(2)}) copy-start(bf16[2,768,256]{2,1,0:T(8,128)(2,1)} %constant.5.clone.c_ref) | copy-start | bytes 2359300
  51.3 1.2 %collective-permute-start.10 = (f32[8,128]{1,0:T(8,128)S(1)}, f32[8,128]{1,0:T(8,128)S(1)}, u32[]{:S(2)}, u32[]{:S(2)}) collective-permute-start(f32[8,128]{1,0:T(8,128)S(1)} %get-tuple-element.28), channel_id=1, source_target_pairs={{0,1},{1,0},{2,3},{3,2},{4,5},{5,4},{6,7},{7,6},{8,9},{9,8},{10,11... | collective-permute-start | bytes 12296 | tf_op jit(solution)/shard_map/ppermute | solution.py:202
  52.5 8.3 %collective-permute-start.13 = (f32[8,128]{1,0:T(8,128)S(1)}, f32[8,128]{1,0:T(8,128)S(1)}, u32[]{:S(2)}, u32[]{:S(2)}) collective-permute-start(f32[8,128]{1,0:T(8,128)S(1)} %add.12), channel_id=1, source_target_pairs={{0,4},{1,5},{2,6},{3,7},{4,0},{5,1},{6,2},{7,3},{8,12},{9,13},{10,... | collective-permute-start | bytes 12296 | tf_op jit(solution)/shard_map/ppermute | solution.py:203
  55.7 5.1 %collective-permute-start.12 = (f32[8,128]{1,0:T(8,128)S(1)}, f32[8,128]{1,0:T(8,128)S(1)}, u32[]{:S(2)}, u32[]{:S(2)}) collective-permute-start(f32[8,128]{1,0:T(8,128)S(1)} %add.12), channel_id=1, source_target_pairs={{0,6},{1,7},{2,0},{3,1},{4,2},{5,3},{6,4},{7,5},{8,14},{9,15},{10,... | collective-permute-start | bytes 12296 | tf_op jit(solution)/shard_map/ppermute | solution.py:203
  56.8 4.8 %collective-permute-start.11 = (f32[8,128]{1,0:T(8,128)S(1)}, f32[8,128]{1,0:T(8,128)S(1)}, u32[]{:S(2)}, u32[]{:S(2)}) collective-permute-start(f32[8,128]{1,0:T(8,128)S(1)} %add.12), channel_id=1, source_target_pairs={{0,2},{1,3},{2,4},{3,5},{4,6},{5,7},{6,0},{7,1},{8,10},{9,11},{10,... | collective-permute-start | bytes 12296 | tf_op jit(solution)/shard_map/ppermute | solution.py:203
